TPU v7x, 32 devices: a whole 2x2x4 slice. The times are simulated.
32 devices in a mesh: req: 4 (over y, core), exp: 8 (over z, x).
Axes of the slice: x: 2, y: 2, z: 4, core: 2. Of those that a mesh axis runs over, the one named last changes fastest.
Arguments:
- residual: bfloat16 [4160, 2048], P(('req', 'exp')), may hold values from -6 to 6
- prefill_qkv: bfloat16 [8, 3, 512, 2048], P('req', None, None, 'exp'), may hold values from -4.5 to 4.5
- decode_qkv: bfloat16 [64, 3, 2048], P('req', None, 'exp'), may hold values from -4.5 to 4.5
- cache_pool: bfloat16 [2, 496, 128, 2048], P(None, 'req', None, 'exp'), may hold values from -4.5 to 4.5
- page_table: int32 [64, 64], P('req'), may hold values from 0 to 123, as said below
- cache_len: int32 [64], P('req'), may hold values from 2 to 8192
- out_weight: bfloat16 [2048, 2048], P('exp'), may hold values from -0.125 to 0.125
- norm_gain: float32 [2048], replicated, may hold values from 0.1 to 1.9
- shared_gate_up: bfloat16 [2, 2048, 5632], P(None, None, 'exp'), may hold values from -0.125 to 0.125
- shared_down: bfloat16 [5632, 2048], P('exp'), may hold values from -0.078125 to 0.078125
- shared_gate: bfloat16 [2048], replicated, may hold values from -0.25 to 0.25
- routes: int32 [4160, 4], P(('req', 'exp')), may hold values from 0 to 31, all different within a row; in each aligned block of 130 rows (0 to 129, 130 to 259, ...) at most 32 rows name the same one
- route_weight: float32 [4160, 4], P(('req', 'exp')), may hold values from 0.1 to 0.5
- expert_gate_up: bfloat16 [32, 2, 2048, 1408], P(('req', 'exp')), may hold values from -0.125 to 0.125
- expert_down: bfloat16 [32, 1408, 2048], P(('req', 'exp')), may hold values from -0.15625 to 0.15625
Outputs:
- layer_out: bfloat16 [4160, 2048], P(('req', 'exp'))
Inputs may be any that keep to these rules, and one draw needn't show every extreme that they name: `page_table`: for decode request i the first ceil(cache_len[i] / 128) entries name distinct pages among the requests of one req index and hold its cache in order; later entries name pages but are not read. `routes`: in the rows of one device (aligned blocks of 130 rows) no expert is named more than 32 times; a row names 4 different experts.
All inputs are finite; a program needn't handle non-finite values.
Results may differ from a plain program's by a relative error of at most 0.015.
Values may be sent and summed in bfloat16 or wider, within the bound.
A program may use at most 128 MiB of HBM per device.

v0:
```python
import jax
import jax.numpy as jnp
from jax import lax
from jax.sharding import PartitionSpec as P

HD = 128
EXP_COL = 4


NEG_FILL = -1e30


def masked_weights(scores, allowed):
    masked = jnp.where(allowed, scores, NEG_FILL)
    highest = jnp.max(masked, axis=-1, keepdims=True)
    raised = jnp.where(allowed, jnp.exp(masked - highest), 0.0)
    return (raised / jnp.sum(raised, axis=-1, keepdims=True)).astype(jnp.bfloat16)


def prefill_heads(prefill_qkv):
    spans, three_rows, span_len, width_here = prefill_qkv.shape
    heads_here = width_here // HD
    split_qkv = prefill_qkv.reshape(spans, three_rows, span_len, heads_here, HD)
    scores = jnp.einsum(
        "pqhd,pkhd->phqk", split_qkv[:, 0], split_qkv[:, 1], preferred_element_type=jnp.float32
    ) * HD ** (-0.5)
    causal = jnp.arange(span_len)[:, None] >= jnp.arange(span_len)[None, :]
    weights = masked_weights(scores, causal[None, None])
    mixed_rows = jnp.einsum(
        "phqk,pkhd->pqhd", weights, split_qkv[:, 2], preferred_element_type=jnp.float32
    )
    return mixed_rows.astype(jnp.bfloat16).reshape(spans * span_len, width_here)


def decode_heads(decode_qkv, cache_pool, page_table, cache_len):
    requests, three_rows, width_here = decode_qkv.shape
    heads_here = width_here // HD
    pool_pages, page_len = (cache_pool.shape[1], cache_pool.shape[2])
    max_pages = page_table.shape[1]
    used_pages = (cache_len + page_len - 1) // page_len
    columns = jnp.broadcast_to(
        jnp.arange(max_pages, dtype=jnp.int32)[None, :], (requests, max_pages)
    )
    live_entry = columns < used_pages[:, None]
    target = jnp.where(live_entry, page_table, pool_pages).reshape(-1)
    request_ids = jnp.broadcast_to(
        jnp.arange(requests, dtype=jnp.int32)[:, None], (requests, max_pages)
    ).reshape(-1)
    owners = jnp.full((pool_pages,), -1, jnp.int32).at[target].set(request_ids, mode="drop")
    page_order = (
        jnp.zeros((pool_pages,), jnp.int32).at[target].set(columns.reshape(-1), mode="drop")
    )
    token_owner = jnp.repeat(owners, page_len)
    token_place = (
        page_order[:, None] * page_len + jnp.arange(page_len, dtype=jnp.int32)[None, :]
    ).reshape(-1)
    allowed = (token_owner[None, :] == jnp.arange(requests, dtype=jnp.int32)[:, None]) & (
        token_place[None, :] < cache_len[:, None]
    )
    pool_rows = cache_pool.reshape(2, pool_pages * page_len, heads_here, HD)
    query_rows = decode_qkv[:, 0].reshape(requests, heads_here, HD)
    own_keys = decode_qkv[:, 1].reshape(requests, heads_here, HD)
    own_values = decode_qkv[:, 2].reshape(requests, heads_here, HD)
    cached = jnp.einsum(
        "ihd,thd->iht", query_rows, pool_rows[0], preferred_element_type=jnp.float32
    ) * HD ** (-0.5)
    own_scores = jnp.einsum(
        "ihd,ihd->ih", query_rows, own_keys, preferred_element_type=jnp.float32
    )[..., None] * HD ** (-0.5)
    joined = jnp.concatenate([cached, own_scores], axis=-1)
    allowed_all = jnp.concatenate(
        [
            jnp.broadcast_to(allowed[:, None, :], cached.shape),
            jnp.ones((requests, heads_here, 1), bool),
        ],
        axis=-1,
    )
    weights = masked_weights(joined, allowed_all)
    mixed_rows = jnp.einsum(
        "iht,thd->ihd", weights[..., :-1], pool_rows[1], preferred_element_type=jnp.float32
    )
    mixed_rows = mixed_rows + weights[..., -1:].astype(jnp.float32) * own_values.astype(jnp.float32)
    return mixed_rows.astype(jnp.bfloat16).reshape(requests, width_here)


def on_device(
    residual,
    prefill_qkv,
    decode_qkv,
    cache_pool,
    page_table,
    cache_len,
    out_weight,
    norm_gain,
    shared_gate_up,
    shared_down,
    shared_gate,
    routes,
    route_weight,
    expert_gate_up,
    expert_down,
):
    attended = jnp.concatenate(
        [prefill_heads(prefill_qkv), decode_heads(decode_qkv, cache_pool, page_table, cache_len)],
        axis=0,
    )
    groups = lax.axis_size("exp")
    tok_rows = residual.shape[0]
    model_width = out_weight.shape[1]
    regrouped = lax.all_to_all(attended, "exp", split_axis=0, concat_axis=1, tiled=True)
    projected = jnp.dot(
        regrouped,
        lax.all_gather(out_weight, "exp", axis=0, tiled=True),
        preferred_element_type=jnp.float32,
    )
    stream = lax.optimization_barrier(
        (residual.astype(jnp.float32) + projected).astype(jnp.bfloat16)
    )
    stream_wide = stream.astype(jnp.float32)
    normed = (
        stream_wide
        * lax.rsqrt(jnp.mean(stream_wide * stream_wide, axis=-1, keepdims=True) + 1e-06)
        * norm_gain
    ).astype(jnp.bfloat16)
    block_rows = lax.all_gather(normed, "exp", axis=0, tiled=True)
    gate_part = jnp.dot(block_rows, shared_gate_up[0], preferred_element_type=jnp.float32)
    up_part = jnp.dot(block_rows, shared_gate_up[1], preferred_element_type=jnp.float32)
    hidden = (jax.nn.silu(gate_part) * up_part).astype(jnp.bfloat16)
    partials = jnp.dot(hidden, shared_down, preferred_element_type=jnp.float32)
    shared = lax.psum_scatter(
        partials.astype(jnp.bfloat16), "exp", scatter_dimension=0, tiled=True
    ).astype(jnp.float32)
    shared_scale = jax.nn.sigmoid(jnp.dot(normed, shared_gate, preferred_element_type=jnp.float32))
    experts_all = EXP_COL * groups
    halves = lax.axis_size("req") // EXP_COL
    route_count = routes.shape[1]
    capacity = max(2, tok_rows * route_count * 2 // experts_all)
    flat_routes = routes.reshape(-1)
    onehot = (flat_routes[:, None] == jnp.arange(experts_all, dtype=jnp.int32)[None, :]).astype(
        jnp.int32
    )
    slot_rank = jnp.sum(onehot * (jnp.cumsum(onehot, axis=0) - 1), axis=1)
    slot_of = flat_routes * capacity + slot_rank
    select = jnp.any(
        jnp.arange(experts_all * capacity, dtype=jnp.int32)[:, None, None]
        == slot_of.reshape(tok_rows, route_count)[None],
        axis=-1,
    ).astype(jnp.bfloat16)
    packed = jnp.dot(select, normed, preferred_element_type=jnp.float32).astype(jnp.bfloat16)
    outgoing = jnp.broadcast_to(
        packed.reshape(experts_all, 1, capacity, model_width),
        (experts_all, halves, capacity, model_width),
    ).reshape(experts_all * halves, capacity, model_width)
    arrived = lax.all_to_all(outgoing, ("req", "exp"), split_axis=0, concat_axis=0, tiled=True)
    senders, slot_total, width_here = arrived.shape
    flat_rows = arrived.reshape(senders * slot_total, width_here)
    expert_gate = jnp.dot(flat_rows, expert_gate_up[0, 0], preferred_element_type=jnp.float32)
    expert_up = jnp.dot(flat_rows, expert_gate_up[0, 1], preferred_element_type=jnp.float32)
    hidden = (jax.nn.silu(expert_gate) * expert_up).astype(jnp.bfloat16)
    answer = jnp.dot(hidden, expert_down[0], preferred_element_type=jnp.float32).astype(
        jnp.bfloat16
    )
    returned = lax.all_to_all(
        answer.reshape(senders, slot_total, width_here),
        ("req", "exp"),
        split_axis=0,
        concat_axis=0,
        tiled=True,
    )
    summed = jnp.sum(
        returned.reshape(experts_all, halves, capacity, model_width).astype(jnp.float32), axis=1
    ).reshape(experts_all * capacity, model_width)
    picked = summed[slot_of].reshape(tok_rows, route_count, model_width)
    routed = jnp.sum(picked * route_weight[..., None], axis=1)
    result_rows = stream_wide + routed + shared_scale[:, None] * shared
    return result_rows.astype(jnp.bfloat16)


def solution(mesh):
    placed = (
        P(("req", "exp"), None),
        P("req", None, None, "exp"),
        P("req", None, "exp"),
        P(None, "req", None, "exp"),
        P("req", None),
        P("req"),
        P("exp", None),
        P(),
        P(None, None, "exp"),
        P("exp", None),
        P(),
        P(("req", "exp"), None),
        P(("req", "exp"), None),
        P(("req", "exp"), None, None, None),
        P(("req", "exp"), None, None),
    )
    return jax.shard_map(
        on_device, mesh=mesh, in_specs=placed, out_specs=P(("req", "exp"), None), check_vma=False
    )
```

profile of v0, /device:TPU:3, one launch (start us, length us, event | category | flops | bytes accessed | tf_op | source)
XLA Modules:
  0.0 550.4 jit_solution(8274325181698577980)
XLA Ops:
  10.1 11.7 %fusion.82 = (bf16[1,124,128,256]{3,2,1,0:T(8,128)(2,1)}, bf16[1,124,128,256]{3,2,1,0:T(8,128)(2,1)}) fusion(bf16[2,124,128,256]{3,2,1,0:T(8,128)(2,1)} %param.18), kind=kLoop, calls=%fused_computation.117 | loop fusion | bytes 32505856 | tf_op jit(solution)/shard_map/slice | solution.py:65
  21.9 16.0 %reshape.261 = bf16[15872,2,128]{2,1,0:T(2,128)(2,1)} reshape(bf16[1,124,128,256]{3,2,1,0:T(8,128)(2,1)} %get-tuple-element.5) | data formatting | bytes 16252928 | tf_op jit(solution)/shard_map/squeeze | solution.py:65
  37.8 16.0 %reshape.262 = bf16[15872,2,128]{2,1,0:T(2,128)(2,1)} reshape(bf16[1,124,128,256]{3,2,1,0:T(8,128)(2,1)} %get-tuple-element.6) | data formatting | bytes 16252928 | tf_op jit(solution)/shard_map/squeeze | solution.py:80
  53.8 4.3 scatter_custom_fusion.1
  58.1 4.8 scatter_custom_fusion
  63.1 6.0 %fusion.2 = f32[16,2,15872]{2,0,1:T(8,128)S(1)} fusion(bf16[15872,2,128]{2,1,0:T(2,128)(2,1)} %reshape.261, bf16[16,2,128]{2,1,0:T(2,128)(2,1)S(1)} %reshape_squeeze.7), kind=kOutput, calls=%fused_computation.5 | convolution fusion | flops 130531328 | bytes 10166272 | tf_op jit(solution)/shard_map/ihd,thd->iht/dot_general | solution.py:64
  74.1 2.7 copy.60
  78.8 2.4 fusion.83
  81.2 2.0 fusion.39
  84.8 5.8 %all-to-all-start = ((bf16[8,130,256]{2,1,0:T(8,128)(2,1)}), bf16[8,130,256]{2,1,0:T(8,128)(2,1)S(1)}, u32[]{:S(2)}, u32[]{:S(2)}) async-start(bf16[8,130,256]{2,1,0:T(8,128)(2,1)} %all_to_all.20), calls=%async_computation | async-start | bytes 1114112 | tf_op jit(solution)/shard_map/all_to_all | solution.py:110
  92.1 3.0 reduce-window.6
  97.1 2.2 fusion.32
  99.3 21.3 %all-to-all-done = bf16[8,130,256]{2,1,0:T(8,128)(2,1)S(1)} async-done(((bf16[8,130,256]{2,1,0:T(8,128)(2,1)}), bf16[8,130,256]{2,1,0:T(8,128)(2,1)S(1)}, u32[]{:S(2)}, u32[]{:S(2)}) %all-to-all-start) | async-done | bytes 532512 | tf_op jit(solution)/shard_map/all_to_all | solution.py:110
  121.7 23.5 %all-gather.4.cloned.1.call-done = bf16[2048,2048]{1,0:T(8,128)(2,1)} async-done(((bf16[256,2048]{1,0:T(8,128)(2,1)}), bf16[2048,2048]{1,0:T(8,128)(2,1)}) %all-gather.4.cloned.1.call-update) | async-done | bytes 8388624 | tf_op jit(solution)/shard_map/all_gather | solution.py:113
  145.2 5.0 fusion.31
  150.4 3.5 convolution_convert_fusion.1
  153.9 4.3 all-to-all-start.1
  159.2 146.7 %all-to-all-done.1 = bf16[32,32,2048]{2,1,0:T(8,128)(2,1)} async-done(((bf16[32,32,2048]{2,1,0:T(8,128)(2,1)}), bf16[32,32,2048]{2,1,0:T(8,128)(2,1)}, u32[]{:S(2)}, u32[]{:S(2)}) %all-to-all-start.1) | async-done | bytes 4194336 | tf_op jit(solution)/shard_map/all_to_all | solution.py:154
  305.9 11.7 %fusion.10 = f32[1024,1408]{1,0:T(8,128)} fusion(bf16[1024,2048]{1,0:T(8,128)(2,1)} %bitcast.14, bf16[1,2,2048,1408]{3,2,1,0:T(8,128)(2,1)} %param.28), kind=kOutput, calls=%fused_computation.14 | convolution fusion | flops 5905580032 | bytes 15728640 | tf_op jit(solution)/shard_map/dot_general | solution.py:157
  317.7 20.6 %fusion.18 = bf16[1024,2048]{1,0:T(8,128)(2,1)} fusion(bf16[1,1408,2048]{2,1,0:T(8,128)(2,1)} %param.29, f32[1024,1408]{1,0:T(8,128)} %fusion.10, bf16[1024,2048]{1,0:T(8,128)(2,1)} %bitcast.14, bf16[1,2,2048,1408]{3,2,1,0:T(8,128)(2,1)} %param.28), kind=kOutput, calls=%fused_computation.26 | convolution fusion | flops 11821907968 | bytes 25690112 | tf_op jit(solution)/shard_map/dot_general | solution.py:160
  338.3 5.1 all-to-all-start.2
  345.4 4.2 reshape.255
  349.6 8.3 %fusion.26 = f32[1040,704]{1,0:T(8,128)} fusion(bf16[1040,2048]{1,0:T(8,128)(2,1)} %reshape.255, bf16[2,2048,704]{1,2,0:T(8,128)(2,1)} %param.23), kind=kOutput, calls=%fused_computation.30 | convolution fusion | flops 2998927360 | bytes 10072064 | tf_op jit(solution)/shard_map/dot_general | solution.py:126
  357.9 12.5 %convolution_convert_fusion = bf16[1040,2048]{1,0:T(8,128)(2,1)} fusion(bf16[704,2048]{1,0:T(8,128)(2,1)S(1)} %copy-done, bf16[1040,2048]{1,0:T(8,128)(2,1)} %reshape.255, f32[1040,704]{1,0:T(8,128)} %fusion.26, bf16[2,2048,704]{1,2,0:T(8,128)(2,1)} %param.23), kind=kOutput, calls=%fused_computation.9 | convolution fusion | flops 6004377600 | bytes 17481728 | tf_op jit(solution)/shard_map/dot_general | solution.py:129
  370.3 122.6 %fusion = bf16[136,2048]{1,0:T(8,128)(2,1)} fusion(bf16[1040,2048]{1,0:T(8,128)(2,1)} %convolution_convert_fusion), kind=kCustom, calls=%all-reduce-scatter | all-reduce-scatter fusion | flops 2228225 | bytes 4817408
  493.9 12.6 %collective-permute-start = (bf16[42,2048]{1,0:T(8,128)(2,1)S(1)}, bf16[42,2048]{1,0:T(8,128)(2,1)}, u32[]{:S(2)}, u32[]{:S(2)}) collective-permute-start(bf16[42,2048]{1,0:T(8,128)(2,1)S(1)} %slice.79), channel_id=1, source_target_pairs={{0,1},{1,2},{2,3},{3,4},{4,5},{5,6},{6,7},{8,9},{9,10},{10,11},{11... | collective-permute-start | bytes 516104
  506.5 2.3 collective-permute-done
  508.9 5.9 %concatenate.12 = bf16[178,2048]{1,0:T(8,128)(2,1)} concatenate(bf16[42,2048]{1,0:T(8,128)(2,1)} %collective-permute-done, bf16[136,2048]{1,0:T(8,128)(2,1)} %fusion), dimensions={0} | concatenate | bytes 1458176
  514.7 6.5 %bitcast_convert_fusion = f32[1024,2048]{1,0:T(8,128)} fusion(bf16[32,32,2048]{2,1,0:T(8,128)(2,1)} %all-to-all-done.2), kind=kLoop, calls=%fused_computation.20 | loop fusion | flops 2097152 | bytes 12582912 | tf_op jit(solution)/shard_map/reshape | solution.py:172
  521.2 9.9 %gather_fusion = f32[520,2048]{1,0:T(8,128)} fusion(f32[1024,2048]{1,0:T(8,128)} %bitcast_convert_fusion, s32[1024]{0:T(1024)S(1)} %pad_clamp_fusion), kind=kCustom, calls=%fused_computation | custom fusion | bytes 8521760 | tf_op jit(solution)/shard_map/gather | solution.py:173
  531.1 5.5 %reshape.224 = f32[130,4,2048]{2,1,0:T(4,128)} reshape(f32[520,2048]{1,0:T(8,128)} %gather_fusion) | data formatting | bytes 8519680 | tf_op jit(solution)/shard_map/reshape | solution.py:173
  536.6 5.5 %multiply_reduce_fusion = f32[130,2048]{1,0:T(8,128)S(1)} fusion(f32[130,4,2048]{2,1,0:T(4,128)} %reshape.224, f32[130,4]{1,0:T(8,128)S(1)} %copy.79), kind=kLoop, calls=%fused_computation.19 | loop fusion | flops 1863680 | bytes 5326880 | tf_op jit(solution)/shard_map/reduce_sum | solution.py:174
  (86 shorter events, 21.4 us)
Async XLA Ops:
  6.5 351.3 %copy-start = (bf16[704,2048]{1,0:T(8,128)(2,1)S(1)}, bf16[704,2048]{1,0:T(8,128)(2,1)}, u32[]{:S(2)}) copy-start(bf16[704,2048]{1,0:T(8,128)(2,1)} %param.24) | copy-start | bytes 8650756
  6.5 138.7 %all-gather.4.cloned.1.call-start = ((), (), s32[]{:S(2)}) async-start(), calls=%async_computation.3 | async-start | bytes 9437184 | tf_op jit(solution)/shard_map/all_gather | solution.py:113
  63.0 6.1 %copy-start.9 = (s32[16]{0:T(128)S(1)}, s32[16]{0:T(128)}, u32[]{:S(2)}) copy-start(s32[16]{0:T(128)} %param.20) | copy-start | bytes 196
  69.5 3.3 copy-start.1
  83.2 7.5 %copy-start.6 = (s32[130,4]{0,1:T(4,128)S(1)}, s32[130,4]{0,1:T(4,128)}, u32[]{:S(2)}) copy-start(s32[130,4]{0,1:T(4,128)} %param.26) | copy-start | bytes 6244
  84.8 35.8 %all-to-all-start = ((bf16[8,130,256]{2,1,0:T(8,128)(2,1)}), bf16[8,130,256]{2,1,0:T(8,128)(2,1)S(1)}, u32[]{:S(2)}, u32[]{:S(2)}) async-start(bf16[8,130,256]{2,1,0:T(8,128)(2,1)} %all_to_all.20), calls=%async_computation | async-start | bytes 1114112 | tf_op jit(solution)/shard_map/all_to_all | solution.py:110
  90.8 0.6 copy-start.4
  145.2 5.2 copy-start.3
  145.2 5.2 copy-start.5
  153.9 152.1 %all-to-all-start.1 = ((bf16[32,32,2048]{2,1,0:T(8,128)(2,1)}), bf16[32,32,2048]{2,1,0:T(8,128)(2,1)}, u32[]{:S(2)}, u32[]{:S(2)}) async-start(bf16[32,32,2048]{2,1,0:T(8,128)(2,1)} %bitcast.114), calls=%async_computation.1 | async-start | bytes 8388608 | tf_op jit(solution)/shard_map/all_to_all | solution.py:154
  158.1 187.2 %all-gather.6.cloned.1.call-start = ((), (), s32[]{:S(2)}) async-start(), calls=%async_computation.4 | async-start | bytes 5013504 | tf_op jit(solution)/shard_map/all_gather | solution.py:125
  338.3 5.1 copy-start.7
  338.3 5.2 copy-start.8
  338.3 5.3 copy-start.10
  338.3 176.5 %all-to-all-start.2 = ((bf16[32,32,2048]{2,1,0:T(8,128)(2,1)}), bf16[32,32,2048]{2,1,0:T(8,128)(2,1)}, u32[]{:S(2)}, u32[]{:S(2)}) async-start(bf16[32,32,2048]{2,1,0:T(8,128)(2,1)} %bitcast.117), calls=%async_computation.2 | async-start | bytes 8388608 | tf_op jit(solution)/shard_map/all_to_all | solution.py:163
  493.9 14.9 %collective-permute-start = (bf16[42,2048]{1,0:T(8,128)(2,1)S(1)}, bf16[42,2048]{1,0:T(8,128)(2,1)}, u32[]{:S(2)}, u32[]{:S(2)}) collective-permute-start(bf16[42,2048]{1,0:T(8,128)(2,1)S(1)} %slice.79), channel_id=1, source_target_pairs={{0,1},{1,2},{2,3},{3,4},{4,5},{5,6},{6,7},{8,9},{9,10},{10,11},{11... | collective-permute-start | bytes 516104
  536.6 5.6 %copy-start.2 = (bf16[178,2048]{1,0:T(8,128)(2,1)S(1)}, bf16[178,2048]{1,0:T(8,128)(2,1)}, u32[]{:S(2)}) copy-start(bf16[178,2048]{1,0:T(8,128)(2,1)} %concatenate.12) | copy-start | bytes 2187268
Sparse Core Ops, SparseCore 0:
  9.5 135.6 all-gather.3
  161.2 137.5 all-gather.5
where the time goes:
time: 561 us; the launch traced here: 550 us
  waiting for transfers between devices  195 us (35%)
  blocking collectives  123 us (22%)
  local copies, waits for them, and re-layouts  89 us (16%)
  matrix products  73.1 us (13%)
  other arithmetic  28.6 us (5%)
  starting transfers between devices  27.8 us (5%)
  between operations  14.7 us (3%)
    all_to_all x1, waiting for transfers between devices, on_device(): lax.all_to_all(outgoing, ('req', 'exp'), split_axis=0, concat_axis=0, til...  147 us
    unnamed x1, blocking collectives  123 us
    all_gather x1, waiting for transfers between devices, on_device(): lax.all_gather(out_weight, 'exp', axis=0, tiled=True)  23.5 us
    all_to_all x1, waiting for transfers between devices, on_device(): lax.all_to_all(attended, 'exp', split_axis=0, concat_axis=1, tiled=True)  21.3 us
    dot_general x1, matrix products, on_device(): jnp.dot(hidden, expert_down[0], preferred_element_type=jnp.float32)  20.6 us
    unnamed x34, local copies, waits for them, and re-layouts  17.6 us
    squeeze x1, local copies, waits for them, and re-layouts, decode_heads(): pool_rows[0]  16 us
    squeeze x1, local copies, waits for them, and re-layouts, decode_heads(): pool_rows[1]  16 us
  transfers between devices with their start and end apart: 6, of which 4 were waited for; matrix products, arithmetic and copies ran while one was open for 50% of the time, Pallas kernels for 0%

commit v1 on v0

v1 whole, which is shorter than its diff:
```python
import functools

import jax
import jax.numpy as jnp
from jax import lax
from jax.experimental import pallas as pl
from jax.experimental.pallas import tpu as pltpu
from jax.sharding import PartitionSpec as P

HD = 128
EXP_COL = 4
ROW_TILE = 16


NEG_FILL = -1e30
ROWS_BY_ROWS = (((1,), (1,)), ((), ()))


def attention_kernel(
    heads, q_ref, k_ref, v_ref, dq_ref, dk_ref, dv_ref, code_ref, ck_ref, cv_ref, out_ref,
    high_ref, sum_ref, acc_ref,
):
    step = pl.program_id(0)
    scaling = HD ** (-0.5)
    span_len = q_ref.shape[2]
    requests, width = dq_ref.shape
    rows = heads * requests

    query, keys, values = (q_ref[0, 0], k_ref[0, 0], v_ref[0, 0])
    half = span_len // 2
    base = pl.multiple_of((step // heads) * span_len, span_len)
    lane = pl.multiple_of((step % heads) * HD, HD)
    for lower, upper in ((0, half), (half, span_len)):
        scores = lax.dot_general(
            query[lower:upper], keys[:upper], ROWS_BY_ROWS, preferred_element_type=jnp.float32
        ) * scaling
        row = lax.broadcasted_iota(jnp.int32, scores.shape, 0) + lower
        column = lax.broadcasted_iota(jnp.int32, scores.shape, 1)
        scores = jnp.where(row >= column, scores, NEG_FILL)
        raised = jnp.exp(scores - jnp.max(scores, axis=-1, keepdims=True))
        total = jnp.sum(raised, axis=-1, keepdims=True)
        mixed = jnp.dot(
            raised.astype(jnp.bfloat16), values[:upper], preferred_element_type=jnp.float32
        )
        out_ref[pl.ds(base + lower, upper - lower), pl.ds(lane, HD)] = (mixed / total).astype(
            out_ref.dtype
        )

    head_of = lax.broadcasted_iota(jnp.int32, (rows, width), 0) // requests
    lane_head = lax.broadcasted_iota(jnp.int32, (rows, width), 1) // HD
    queries = jnp.where(
        head_of == lane_head,
        jnp.concatenate([dq_ref[...].astype(jnp.float32)] * heads, axis=0),
        0.0,
    )

    @pl.when(step == 0)
    def _():
        own = jnp.concatenate([dk_ref[...].astype(jnp.float32)] * heads, axis=0)
        high_ref[...] = jnp.sum(queries * own, axis=-1, keepdims=True) * scaling
        sum_ref[...] = jnp.ones_like(sum_ref)
        acc_ref[...] = jnp.concatenate([dv_ref[...].astype(jnp.float32)] * heads, axis=0)

    scores = lax.dot_general(
        queries.astype(jnp.bfloat16), ck_ref[0], ROWS_BY_ROWS, preferred_element_type=jnp.float32
    ) * scaling
    request = lax.broadcasted_iota(jnp.int32, scores.shape, 0) % requests
    allowed = request == code_ref[...]
    scores = jnp.where(allowed, scores, NEG_FILL)
    before = high_ref[...]
    after = jnp.maximum(before, jnp.max(scores, axis=-1, keepdims=True))
    raised = jnp.where(allowed, jnp.exp(scores - after), 0.0)
    fade = jnp.exp(before - after)
    high_ref[...] = after
    sum_ref[...] = sum_ref[...] * fade + jnp.sum(raised, axis=-1, keepdims=True)
    acc_ref[...] = acc_ref[...] * fade + jnp.dot(
        raised.astype(jnp.bfloat16), cv_ref[0], preferred_element_type=jnp.float32
    )

    @pl.when(step == pl.num_programs(0) - 1)
    def _():
        mixed = acc_ref[...] / sum_ref[...]
        first = out_ref.shape[0] - requests
        for head in range(heads):
            lanes = slice(head * HD, (head + 1) * HD)
            out_ref[first:, lanes] = mixed[
                head * requests : (head + 1) * requests, lanes
            ].astype(out_ref.dtype)


def attend(prefill_qkv, decode_qkv, cache_pool, page_table, cache_len):
    spans, _, span_len, width = prefill_qkv.shape
    requests = decode_qkv.shape[0]
    heads = width // HD
    steps = spans * heads
    pool_pages, page_len = (cache_pool.shape[1], cache_pool.shape[2])
    max_pages = page_table.shape[1]
    chunk = pool_pages // steps * page_len
    order = jnp.arange(max_pages, dtype=jnp.int32)
    left = cache_len[:, None] - order[None, :] * page_len
    held = (page_table[None] == jnp.arange(pool_pages, dtype=jnp.int32)[:, None, None]) & (
        left > 0
    )[None]
    owner = jnp.max(
        jnp.where(held, jnp.arange(requests, dtype=jnp.int32)[None, :, None], -1), axis=(1, 2)
    )
    valid = jnp.max(jnp.where(held, left[None], 0), axis=(1, 2))
    code = jnp.where(
        jnp.arange(page_len, dtype=jnp.int32)[None, :] < valid[:, None], owner[:, None], -1
    ).reshape(1, pool_pages * page_len)
    pool = cache_pool.reshape(2, pool_pages * page_len, width)
    whole = pl.BlockSpec((requests, width), lambda g: (0, 0))
    part = [
        pl.BlockSpec((1, 1, span_len, HD), functools.partial(lambda j, g: (g // heads, j, 0, g % heads), j))
        for j in range(3)
    ]
    out_rows = spans * span_len + requests
    return pl.pallas_call(
        functools.partial(attention_kernel, heads),
        grid=(steps,),
        in_specs=part
        + [whole] * 3
        + [
            pl.BlockSpec((1, chunk), lambda g: (0, g)),
            pl.BlockSpec((1, chunk, width), lambda g: (0, g, 0)),
            pl.BlockSpec((1, chunk, width), lambda g: (1, g, 0)),
        ],
        out_specs=pl.BlockSpec((out_rows, width), lambda g: (0, 0)),
        out_shape=jax.ShapeDtypeStruct((out_rows, width), jnp.bfloat16),
        scratch_shapes=[
            pltpu.VMEM((heads * requests, 1), jnp.float32),
            pltpu.VMEM((heads * requests, 1), jnp.float32),
            pltpu.VMEM((heads * requests, width), jnp.float32),
        ],
        compiler_params=pltpu.CompilerParams(vmem_limit_bytes=40 * 2**20),
        cost_estimate=pl.CostEstimate(
            flops=2 * 10**9, bytes_accessed=2 * pool.size + 2 * prefill_qkv.size, transcendentals=2 * 10**6
        ),
    )(
        prefill_qkv, prefill_qkv, prefill_qkv,
        decode_qkv[:, 0], decode_qkv[:, 1], decode_qkv[:, 2],
        code, pool, pool,
    )


LINE = 4
MESH = pl.DeviceIdType.MESH


def greet(place, line, groups, columns):
    outer, inner = place
    long, short = line
    barrier = pltpu.get_barrier_semaphore()
    count = jnp.int32(0)
    for ok, target in (
        (outer > 0, (outer - 1) * short + inner),
        (outer < long - 1, (outer + 1) * short + inner),
        (inner > 0, outer * short + inner - 1),
        (inner < short - 1, outer * short + inner + 1),
    ):
        @pl.when(ok)
        def _():
            pl.semaphore_signal(barrier, inc=1, device_id={"exp": target}, device_id_type=MESH)

        count = count + ok.astype(jnp.int32)
    if columns > 1:
        me = lax.axis_index("req")
        for k in range(1, columns):
            pl.semaphore_signal(
                barrier, inc=1, device_id={"req": (me + k) % columns}, device_id_type=MESH
            )
        count = count + (columns - 1)
    pl.semaphore_wait(barrier, count)


def visit(place, long, farthest_first, body):
    outer = place[0]
    distances = range(long - 1, -1, -1) if farthest_first else range(long)
    for distance in distances:
        @pl.when(outer + distance < long)
        def _():
            body(outer + distance, distance, 0)

        if distance > 0:
            @pl.when(outer - distance >= 0)
            def _():
                body(outer - distance, distance, 1)


def reduce_scatter(place, line, part, fill, column, rin, rout, total, sems):
    outer, inner = place
    long, short = line
    isend, irecv, osend, orecv = sems

    def inner_copy(way, o, i, relay):
        target = outer * short + inner + (1 if way == 0 else -1)
        return pltpu.make_async_remote_copy(
            src_ref=(rin.at[way, o, i] if relay else part.at[o, i]),
            dst_ref=rin.at[way, o, i],
            send_sem=isend.at[way, o, i],
            recv_sem=irecv.at[way, o, i],
            device_id={"exp": target},
            device_id_type=MESH,
        )

    def outer_copy(way, o):
        target = (outer + (1 if way == 0 else -1)) * short + inner
        return pltpu.make_async_remote_copy(
            src_ref=column.at[o],
            dst_ref=rout.at[way, o],
            send_sem=osend.at[way, o],
            recv_sem=orecv.at[way, o],
            device_id={"exp": target},
            device_id_type=MESH,
        )

    def first(o, distance, side):
        fill(o)
        for way in (0, 1):
            for gap in range(short - 1, 0, -1):
                i = inner + gap if way == 0 else inner - gap
                ok = (i < short) if way == 0 else (i >= 0)
                behind = (inner > 0) if way == 0 else (inner < short - 1)
                if short == 2:
                    @pl.when(ok)
                    def _():
                        inner_copy(way, o, i, False).start()
                else:
                    @pl.when(ok & jnp.logical_not(behind))
                    def _():
                        inner_copy(way, o, i, False).start()

    visit(place, long, True, first)

    def second(o, distance, side):
        if short > 2:
            for way in (0, 1):
                for gap in range(short - 1, 0, -1):
                    i = inner + gap if way == 0 else inner - gap
                    ok = (i < short) if way == 0 else (i >= 0)
                    behind = (inner > 0) if way == 0 else (inner < short - 1)

                    @pl.when(ok & behind)
                    def _():
                        inner_copy(way, o, i, True).wait_recv()
                        rin[way, o, i] = (
                            rin[way, o, i].astype(jnp.float32) + part[o, i].astype(jnp.float32)
                        ).astype(jnp.bfloat16)
                        inner_copy(way, o, i, True).start()

        total[...] = part[o, inner].astype(jnp.float32)
        for way, behind in ((0, inner > 0), (1, inner < short - 1)):
            @pl.when(behind)
            def _():
                inner_copy(way, o, inner, False).wait_recv()
                total[...] += rin[way, o, inner].astype(jnp.float32)

        for way, behind in ((0, outer > 0), (1, outer < long - 1)):
            if distance == 0 or way == side:
                @pl.when(behind)
                def _():
                    outer_copy(way, o).wait_recv()
                    total[...] += rout[way, o].astype(jnp.float32)

        if distance > 0:
            column[o] = total[...].astype(jnp.bfloat16)
            outer_copy(side, o).start()

    visit(place, long, True, second)

    def finish():
        for o in range(long):
            for i in range(short):
                @pl.when(inner < i)
                def _():
                    inner_copy(0, o, i, False).wait_send()

                @pl.when(inner > i)
                def _():
                    inner_copy(1, o, i, False).wait_send()

            @pl.when(outer < o)
            def _():
                outer_copy(0, o).wait_send()

            @pl.when(outer > o)
            def _():
                outer_copy(1, o).wait_send()

    return finish


def front_kernel(
    line, columns, att_ref, w_ref, res_ref, gain_ref, sel_ref, stream_ref, all_ref, arr_ref,
    part, column, rin, rout, total, pack, isend, irecv, osend, orecv, asend, arecv, ysend, yrecv,
):
    long, short = line
    groups = long * short
    exp = lax.axis_index("exp")
    me = lax.axis_index("req")
    place = (exp // short, exp % short)
    outer, inner = place
    greet(place, line, groups, columns)

    def fill(o):
        for i in range(short):
            part[o, i] = jnp.dot(
                att_ref[o, i], w_ref[...], preferred_element_type=jnp.float32
            ).astype(jnp.bfloat16)

    finish = reduce_scatter(
        place, line, part, fill, column, rin, rout, total, (isend, irecv, osend, orecv)
    )
    stream = (res_ref[...].astype(jnp.float32) + total[...]).astype(jnp.bfloat16)
    stream_ref[...] = stream
    wide = stream.astype(jnp.float32)
    all_ref[outer, inner] = (
        wide
        * lax.rsqrt(jnp.mean(wide * wide, axis=-1, keepdims=True) + 1e-06)
        * gain_ref[...]
    ).astype(jnp.bfloat16)

    def pass_on(way, o, i):
        target = exp + (short, -short, 1, -1)[way]
        return pltpu.make_async_remote_copy(
            src_ref=all_ref.at[o, i],
            dst_ref=all_ref.at[o, i],
            send_sem=asend.at[way, o, i],
            recv_sem=arecv.at[o, i],
            device_id={"exp": target},
            device_id_type=MESH,
        )

    def to_column(k, o, i):
        target = (me + k) % columns
        return pltpu.make_async_remote_copy(
            src_ref=pack.at[o, i, target],
            dst_ref=arr_ref.at[me, o, i],
            send_sem=ysend.at[k, o, i],
            recv_sem=yrecv.at[k, o, i],
            device_id={"req": target},
            device_id_type=MESH,
        )

    def dispatch(o, i):
        rows = jnp.dot(
            sel_ref[o, i], all_ref[o, i], preferred_element_type=jnp.float32
        ).astype(jnp.bfloat16)
        pack[o, i] = rows.reshape(pack.shape[2:])
        for k in range(1, columns):
            to_column(k, o, i).start()
        arr_ref[me, o, i] = pack[o, i, me]

    def spread(o, distance, side):
        if distance > 0:
            pass_on(0, o, inner).wait_recv()
        for way, ahead in ((0, outer < long - 1), (1, outer > 0)):
            if distance == 0 or way == 1 - side:
                @pl.when(ahead)
                def _():
                    pass_on(way, o, inner).start()
        for way, ahead in ((2, inner < short - 1), (3, inner > 0)):
            @pl.when(ahead)
            def _():
                pass_on(way, o, inner).start()
        dispatch(o, inner)

    def across(o, distance, side):
        for gap in range(1, short):
            for way, i, ok, ahead in (
                (2, inner - gap, inner - gap >= 0, inner < short - 1),
                (3, inner + gap, inner + gap < short, inner > 0),
            ):
                @pl.when(ok)
                def _():
                    pass_on(way, o, i).wait_recv()
                    if short > 2:
                        @pl.when(ahead)
                        def _():
                            pass_on(way, o, i).start()
                    dispatch(o, i)

    for step in range(long + 1):
        if step < long:
            near(place, long, step, spread)
        if step > 0:
            near(place, long, step - 1, across)

    finish()
    for o in range(long):
        for i in range(short):
            at_line = inner == i
            @pl.when(at_line & (outer >= o) & (outer < long - 1))
            def _():
                pass_on(0, o, i).wait_send()

            @pl.when(at_line & (outer <= o) & (outer > 0))
            def _():
                pass_on(1, o, i).wait_send()

            @pl.when((inner >= i) & (inner < short - 1))
            def _():
                pass_on(2, o, i).wait_send()

            @pl.when((inner <= i) & (inner > 0))
            def _():
                pass_on(3, o, i).wait_send()

            for k in range(1, columns):
                to_column(k, o, i).wait_send()
                to_column(k, o, i).wait_recv()


def near(place, long, distance, body):
    outer = place[0]

    @pl.when(outer + distance < long)
    def _():
        body(outer + distance, distance, 0)

    if distance > 0:
        @pl.when(outer - distance >= 0)
        def _():
            body(outer - distance, distance, 1)


def front(attended, out_weight, residual, norm_gain, select, line, columns):
    long, short = line
    tokens, width = residual.shape
    depth = out_weight.shape[0]
    rows = select.shape[2] // columns
    dma = pltpu.SemaphoreType.DMA
    block = (long, short, tokens, width)
    vmem = pl.BlockSpec(memory_space=pltpu.VMEM)
    bf16 = jnp.bfloat16
    return pl.pallas_call(
        functools.partial(front_kernel, line, columns),
        out_shape=(
            jax.ShapeDtypeStruct((tokens, width), bf16),
            jax.ShapeDtypeStruct(block, bf16),
            jax.ShapeDtypeStruct((columns, long, short, rows, width), bf16),
        ),
        in_specs=[vmem] * 5,
        out_specs=(vmem, vmem, vmem),
        scratch_shapes=[
            pltpu.VMEM(block, bf16),
            pltpu.VMEM((long, tokens, width), bf16),
            pltpu.VMEM((2,) + block, bf16),
            pltpu.VMEM((2, long, tokens, width), bf16),
            pltpu.VMEM((tokens, width), jnp.float32),
            pltpu.VMEM((long, short, columns, rows, width), bf16),
            dma((2, long, short)),
            dma((2, long, short)),
            dma((2, long)),
            dma((2, long)),
            dma((4, long, short)),
            dma((long, short)),
            dma((columns, long, short)),
            dma((columns, long, short)),
        ],
        compiler_params=pltpu.CompilerParams(
            collective_id=0, has_side_effects=True, vmem_limit_bytes=56 * 2**20
        ),
        cost_estimate=pl.CostEstimate(
            flops=4 * 10**9, bytes_accessed=2 * 10**7, transcendentals=0
        ),
    )(
        attended.reshape(long, short, tokens, depth), out_weight, residual,
        norm_gain.reshape(1, width), select,
    )


def back_kernel(
    line, part_ref, stream_ref, out_ref, column, rin, rout, total, isend, irecv, osend, orecv
):
    exp = lax.axis_index("exp")
    place = (exp // line[1], exp % line[1])
    greet(place, line, line[0] * line[1], 1)
    finish = reduce_scatter(
        place, line, part_ref, lambda o: None, column, rin, rout, total,
        (isend, irecv, osend, orecv),
    )
    out_ref[...] = (stream_ref[...].astype(jnp.float32) + total[...]).astype(jnp.bfloat16)
    finish()


def back(partials, stream, line):
    long, short = line
    tokens, width = stream.shape
    dma = pltpu.SemaphoreType.DMA
    block = (long, short, tokens, width)
    vmem = pl.BlockSpec(memory_space=pltpu.VMEM)
    bf16 = jnp.bfloat16
    return pl.pallas_call(
        functools.partial(back_kernel, line),
        out_shape=jax.ShapeDtypeStruct((tokens, width), bf16),
        in_specs=[vmem] * 2,
        out_specs=vmem,
        scratch_shapes=[
            pltpu.VMEM((long, tokens, width), bf16),
            pltpu.VMEM((2,) + block, bf16),
            pltpu.VMEM((2, long, tokens, width), bf16),
            pltpu.VMEM((tokens, width), jnp.float32),
            dma((2, long, short)),
            dma((2, long, short)),
            dma((2, long)),
            dma((2, long)),
        ],
        compiler_params=pltpu.CompilerParams(
            collective_id=1, has_side_effects=True, vmem_limit_bytes=56 * 2**20
        ),
        cost_estimate=pl.CostEstimate(
            flops=10**7, bytes_accessed=2 * 10**7, transcendentals=0
        ),
    )(partials.reshape(block), stream)


def on_device(
    residual,
    prefill_qkv,
    decode_qkv,
    cache_pool,
    page_table,
    cache_len,
    out_weight,
    norm_gain,
    shared_gate_up,
    shared_down,
    shared_gate,
    routes,
    route_weight,
    expert_gate_up,
    expert_down,
):
    attended = attend(prefill_qkv, decode_qkv, cache_pool, page_table, cache_len)
    groups = lax.axis_size("exp")
    columns = lax.axis_size("req")
    tok_rows = residual.shape[0]
    model_width = out_weight.shape[1]
    line = (LINE, groups // LINE)
    rank_of, weight_of = dispatch_plan(routes, route_weight)
    rows = row_limit(routes.shape, groups)
    select = (
        (jnp.arange(rows, dtype=jnp.int32)[None, None, :, None] == rank_of[:, :, None, :])
        .astype(jnp.bfloat16)
        .reshape(line + (columns * rows, tok_rows))
    )
    stream, gathered, arrived = front(
        attended, out_weight, residual, norm_gain, select, line, columns
    )
    block_rows = gathered.reshape(groups * tok_rows, model_width)
    arrived = arrived.reshape(columns * groups * rows, model_width)

    gate_part = jnp.dot(block_rows, shared_gate_up[0], preferred_element_type=jnp.float32)
    up_part = jnp.dot(block_rows, shared_gate_up[1], preferred_element_type=jnp.float32)
    hidden = (jax.nn.silu(gate_part) * up_part).astype(jnp.bfloat16)
    shared_scale = jax.nn.sigmoid(
        jnp.dot(block_rows, shared_gate, preferred_element_type=jnp.float32)
    )
    shared = jnp.dot(hidden, shared_down, preferred_element_type=jnp.float32)
    shared = shared_scale[:, None] * shared

    expert_gate = jnp.dot(arrived, expert_gate_up[0, 0], preferred_element_type=jnp.float32)
    expert_up = jnp.dot(arrived, expert_gate_up[0, 1], preferred_element_type=jnp.float32)
    hidden = (jax.nn.silu(expert_gate) * expert_up).astype(jnp.bfloat16)
    answer = jnp.dot(hidden, expert_down[0], preferred_element_type=jnp.float32).astype(
        jnp.bfloat16
    )
    returned = lax.all_to_all(answer, "req", split_axis=0, concat_axis=0, tiled=True)
    returned = returned.reshape(columns, groups, rows, model_width)
    spread = jnp.where(
        jnp.arange(rows, dtype=jnp.int32)[None, None, :, None] == rank_of[:, :, None, :],
        weight_of[:, :, None, :],
        0.0,
    ).astype(jnp.bfloat16)
    routed = jnp.einsum("gcrt,cgrd->gtd", spread, returned, preferred_element_type=jnp.float32)
    partials = (shared.reshape(routed.shape) + routed).astype(jnp.bfloat16)
    return back(partials, stream, line)


def row_limit(routes_shape, groups):
    tok_rows, route_count = routes_shape
    return max(2, tok_rows * route_count * 2 // (EXP_COL * groups))


def dispatch_plan(routes, route_weight):
    groups = lax.axis_size("exp")
    columns = lax.axis_size("req")
    halves = columns // EXP_COL
    all_routes = lax.all_gather(routes.T, "exp", axis=0)
    all_weights = lax.all_gather(route_weight.T, "exp", axis=0)
    mine = (jnp.arange(columns, dtype=jnp.int32) * groups + lax.axis_index("exp")) // halves
    onehot = all_routes[:, None] == mine[None, :, None, None]
    named = jnp.any(onehot, axis=2).astype(jnp.int32)
    rank_of = jnp.where(named > 0, jnp.cumsum(named, axis=2) - 1, -1)
    weight_of = jnp.sum(jnp.where(onehot, all_weights[:, None], 0.0), axis=2)
    return rank_of, weight_of


def solution(mesh):
    placed = (
        P(("req", "exp"), None),
        P("req", None, None, "exp"),
        P("req", None, "exp"),
        P(None, "req", None, "exp"),
        P("req", None),
        P("req"),
        P("exp", None),
        P(),
        P(None, None, "exp"),
        P("exp", None),
        P(),
        P(("req", "exp"), None),
        P(("req", "exp"), None),
        P(("req", "exp"), None, None, None),
        P(("req", "exp"), None, None),
    )
    return jax.shard_map(
        on_device, mesh=mesh, in_specs=placed, out_specs=P(("req", "exp"), None), check_vma=False
    )
```

time: 561 us -> 339 us (0.60)
  the two profiles are of different devices: /device:TPU:3 before, /device:TPU:0 now
where the time goes in v1:
time: 339 us
  Pallas kernels  181 us (53%)
  matrix products  64.3 us (19%)
  blocking collectives  63 us (19%)
  local copies, waits for them, and re-layouts  19.3 us (6%)
  other arithmetic  6.48 us (2%)
  starting transfers between devices  5.02 us (1%)
    pallas_call x1, Pallas kernels, front(): pl.pallas_call(functools.partial(front_kernel, line, columns), out_shape=...  113 us
    pallas_call x1, Pallas kernels, back(): pl.pallas_call(functools.partial(back_kernel, line), out_shape=jax.ShapeD...  55.2 us
    all_gather x1, blocking collectives, dispatch_plan(): all_routes = lax.all_gather(routes.T, 'exp', axis=0)  32.3 us
    all_gather x1, blocking collectives, dispatch_plan(): all_weights = lax.all_gather(route_weight.T, 'exp', axis=0)  30.6 us
    dot_general x1, matrix products, on_device(): jnp.dot(hidden, expert_down[0], preferred_element_type=jnp.float32)  20.6 us
    dot_general x1, matrix products, on_device(): shared = jnp.dot(hidden, shared_down, preferred_element_type=jnp.float32)  13 us
    pallas_call x1, Pallas kernels, attend(): pl.pallas_call(functools.partial(attention_kernel, heads), grid=(steps,),...  12.2 us
    dot_general x1, matrix products, on_device(): jnp.dot(arrived, expert_gate_up[0, 0], preferred_element_type=jnp.float32)  11.7 us
  transfers between devices with their start and end apart: 1, of which 0 were waited for; matrix products, arithmetic and copies ran while one was open for 11% of the time, Pallas kernels for 0%

profile of v1, /device:TPU:0, one launch (start us, length us, event | category | flops | bytes accessed | tf_op | source)
XLA Modules:
  0.0 338.9 jit_solution(4672315160854750897)
XLA Ops:
  0.0 0.9 broadcast_compare_fusion
  0.9 0.7 broadcast_subtract_fusion
  1.6 0.1 eq.61
  1.7 0.7 slice_bitcast_fusion
  2.4 32.3 %all-gather.2 = s32[8,4,130]{2,1,0:T(4,128)S(1)} all-gather(s32[1,4,130]{2,1,0:T(4,128)} %bitcast.79), channel_id=2, replica_groups=mesh['req'=4,'exp'=8] {'exp'}, dimensions={0}, use_global_device_ids=true | all-gather | bytes 18720 | tf_op jit(solution)/shard_map/all_gather | solution.py:590
  34.8 0.1 compare_reduce_fusion
  34.9 2.3 reduce-window.6
  37.2 0.3 slice_reduce_fusion
  37.5 0.1 copy_bitcast_fusion.1
  37.6 1.3 select_reduce_fusion.1
  38.9 0.1 select_bitcast_fusion
  39.0 0.1 copy.40
  39.0 0.0 copy-start.1
  39.1 1.4 copy-done.1
  40.5 12.2 %shard_map.145 = bf16[1040,256]{1,0:T(8,128)(2,1)S(1)} custom-call(bf16[2,3,512,256]{3,2,1,0:T(8,128)(2,1)S(1)} %copy-done.1, bf16[2,3,512,256]{3,2,1,0:T(8,128)(2,1)S(1)} %copy-done.1, bf16[2,3,512,256]{3,2,1,0:T(8,128)(2,1)S(1)} %copy-done.1, bf16[16,256]{1,0:T(8,128)(2,1)S(1)} %get-tuple-element.14.dq_ref, bf16[16,256]{1,0:T(8,128)(2,1)S(1)} %get-tuple-element.15.dk_ref, ...), custom_call_target="tpu_custom_call" | custom-call | flops 2000000000 | bytes 17825792 | tf_op jit(solution)/shard_map/pallas_call | solution.py:118
  52.6 0.9 reshape.146.att_ref
  53.6 0.1 eq.66
  53.7 0.9 compare_convert_fusion.sel_ref
  54.6 113.3 %shard_map.146 = (bf16[130,2048]{1,0:T(8,128)(2,1)}, bf16[4,2,130,2048]{3,2,1,0:T(8,128)(2,1)}, bf16[4,4,2,32,2048]{4,3,2,1,0:T(8,128)(2,1)}) custom-call(bf16[4,2,130,256]{3,2,1,0:T(8,128)(2,1)} %reshape.146.att_ref, bf16[256,2048]{1,0:T(8,128)(2,1)} %w_ref.1, bf16[130,2048]{1,0:T(8,128)(2,1)} %res_ref.1, f32[1,2048]{1,0:T(1,128)} %bitcast.81, ...), custom_call_target="tpu_custom_call" | custom-call | flops 4000000000 | bytes 20000000 | tf_op jit(solution)/shard_map/pallas_call | solution.py:436
  167.9 11.7 %fusion.5 = f32[1024,1408]{1,0:T(8,128)} fusion(bf16[1024,2048]{1,0:T(8,128)(2,1)} %bitcast.82, bf16[1,2,2048,1408]{3,2,1,0:T(8,128)(2,1)} %param.28), kind=kOutput, calls=%fused_computation.7 | convolution fusion | flops 5905580032 | bytes 15728640 | tf_op jit(solution)/shard_map/dot_general | solution.py:563
  179.6 20.6 %fusion.14 = bf16[1024,2048]{1,0:T(8,128)(2,1)} fusion(bf16[1,1408,2048]{2,1,0:T(8,128)(2,1)} %param.29, f32[1024,1408]{1,0:T(8,128)} %fusion.5, bf16[1024,2048]{1,0:T(8,128)(2,1)} %bitcast.83, bf16[1,2,2048,1408]{3,2,1,0:T(8,128)(2,1)} %param.28), kind=kOutput, calls=%fused_computation.14 | convolution fusion | flops 11821907968 | bytes 25690112 | tf_op jit(solution)/shard_map/dot_general | solution.py:566
  200.2 5.0 %all-to-all-start = ((bf16[4,256,2048]{2,1,0:T(8,128)(2,1)}), bf16[4,256,2048]{2,1,0:T(8,128)(2,1)}, u32[]{:S(2)}, u32[]{:S(2)}) async-start(bf16[4,256,2048]{2,1,0:T(8,128)(2,1)} %bitcast.77), calls=%async_computation | async-start | bytes 8388608 | tf_op jit(solution)/shard_map/all_to_all | solution.py:569
  205.3 30.6 %all-gather.3 = f32[8,4,130]{2,1,0:T(4,128)S(1)} all-gather(f32[1,4,130]{2,1,0:T(4,128)S(1)} %bitcast.80), channel_id=3, replica_groups=mesh['req'=4,'exp'=8] {'exp'}, dimensions={0}, use_global_device_ids=true | all-gather | bytes 18720 | tf_op jit(solution)/shard_map/all_gather | solution.py:591
  235.9 0.1 fusion.32
  236.0 4.2 %reshape.150 = bf16[1040,2048]{1,0:T(8,128)(2,1)} reshape(bf16[4,2,130,2048]{3,2,1,0:T(8,128)(2,1)} %get-tuple-element.8) | data formatting | bytes 8519680 | tf_op jit(solution)/shard_map/reshape | solution.py:551
  240.2 3.6 %convolution_reduce_fusion = f32[1040]{0:T(1024)S(1)} fusion(bf16[1040,2048]{1,0:T(8,128)(2,1)} %reshape.150, bf16[2048,1]{0,1:T(2,128)(2,1)S(1)} %reshape.163), kind=kOutput, calls=%fused_computation.22 | convolution fusion | flops 4259840 | bytes 4268096 | tf_op jit(solution)/shard_map/dot_general | solution.py:558
  243.8 7.0 %fusion.21 = f32[1040,704]{1,0:T(8,128)} fusion(bf16[1040,2048]{1,0:T(8,128)(2,1)S(1)} %copy-done.2, bf16[2,2048,704]{1,2,0:T(8,128)(2,1)} %param.23), kind=kOutput, calls=%fused_computation.17 | convolution fusion | flops 2998927360 | bytes 10072064 | tf_op jit(solution)/shard_map/dot_general | solution.py:554
  250.9 13.0 %convolution_multiply_fusion = f32[1040,2048]{1,0:T(8,128)} fusion(bf16[704,2048]{1,0:T(8,128)(2,1)S(1)} %copy-done, f32[1040]{0:T(1024)S(1)} %add_divide_fusion, bf16[1040,2048]{1,0:T(8,128)(2,1)} %reshape.150, f32[1040,704]{1,0:T(8,128)} %fusion.21, bf16[2,2048,704]{1,2,0:T(8,128)(2,1)} %param.23), kind=kOutput, calls=%fused_computation | convolution fusion | flops 6004377600 | bytes 21745728 | tf_op jit(solution)/shard_map/dot_general | solution.py:560
  263.9 9.5 %reshape.151 = f32[8,130,2048]{2,1,0:T(8,128)} reshape(f32[1040,2048]{1,0:T(8,128)} %convolution_multiply_fusion) | data formatting | bytes 17039360 | tf_op jit(solution)/shard_map/reshape | solution.py:577
  273.4 8.3 %fusion = bf16[8,130,2048]{2,1,0:T(8,128)(2,1)} fusion(f32[8,130,2048]{2,1,0:T(8,128)} %reshape.151, bf16[4,8,32,2048]{3,2,1,0:T(8,128)(2,1)} %bitcast.17, bf16[8,4,130]{2,1,0:T(4,128)(2,1)S(1)} %copy.29, s32[8,4,130]{2,1,0:T(4,128)S(1)} %copy.27), kind=kOutput, calls=%fused_computation.2 | convolution fusion | flops 549785600 | bytes 16998784 | tf_op jit(solution)/shard_map/gcrt,cgrd->gtd/dot_general | solution.py:576
  281.7 55.2 %shard_map.147 = bf16[130,2048]{1,0:T(8,128)(2,1)} custom-call(bf16[4,2,130,2048]{3,2,1,0:T(8,128)(2,1)} %bitcast.76, bf16[130,2048]{1,0:T(8,128)(2,1)} %get-tuple-element.10.stream_ref), custom_call_target="tpu_custom_call" | custom-call | flops 10000000 | bytes 20000000 | tf_op jit(solution)/shard_map/pallas_call | solution.py:494
  337.0 1.9 copy.42
  (23 shorter events, 0.1 us)
Async XLA Ops:
  0.0 250.9 %copy-start = (bf16[704,2048]{1,0:T(8,128)(2,1)S(1)}, bf16[704,2048]{1,0:T(8,128)(2,1)}, u32[]{:S(2)}) copy-start(bf16[704,2048]{1,0:T(8,128)(2,1)} %param.24) | copy-start | bytes 8650756
  39.0 1.4 copy-start.1
  200.2 5.0 %copy-start.3 = (bf16[2048]{0:T(1024)(128)(2,1)S(1)}, bf16[2048]{0:T(1024)(128)(2,1)}, u32[]{:S(2)}) copy-start(bf16[2048]{0:T(1024)(128)(2,1)} %param.25) | copy-start | bytes 12292
  200.2 5.1 %copy-start.4 = (f32[130,4]{0,1:T(4,128)S(1)}, f32[130,4]{0,1:T(4,128)}, u32[]{:S(2)}) copy-start(f32[130,4]{0,1:T(4,128)} %param.27) | copy-start | bytes 6244
  200.2 73.2 %all-to-all-start = ((bf16[4,256,2048]{2,1,0:T(8,128)(2,1)}), bf16[4,256,2048]{2,1,0:T(8,128)(2,1)}, u32[]{:S(2)}, u32[]{:S(2)}) async-start(bf16[4,256,2048]{2,1,0:T(8,128)(2,1)} %bitcast.77), calls=%async_computation | async-start | bytes 8388608 | tf_op jit(solution)/shard_map/all_to_all | solution.py:569
  240.2 3.6 %copy-start.2 = (bf16[1040,2048]{1,0:T(8,128)(2,1)S(1)}, bf16[1040,2048]{1,0:T(8,128)(2,1)}, u32[]{:S(2)}) copy-start(bf16[1040,2048]{1,0:T(8,128)(2,1)} %reshape.150) | copy-start | bytes 12779524

commit v2 on v1

--- a/solution.py
+++ b/solution.py
@@ -147,12 +147,19 @@
 MESH = pl.DeviceIdType.MESH
 
 
-def greet(place, line, groups, columns):
+def greet(place, line, groups, columns, all_groups):
     outer, inner = place
     long, short = line
     barrier = pltpu.get_barrier_semaphore()
     count = jnp.int32(0)
-    for ok, target in (
+    if all_groups:
+        exp = outer * short + inner
+        for k in range(1, groups):
+            pl.semaphore_signal(
+                barrier, inc=1, device_id={"exp": (exp + k) % groups}, device_id_type=MESH
+            )
+        count = count + (groups - 1)
+    for ok, target in () if all_groups else (
         (outer > 0, (outer - 1) * short + inner),
         (outer < long - 1, (outer + 1) * short + inner),
         (inner > 0, outer * short + inner - 1),
@@ -290,9 +297,31 @@
     return finish
 
 
+def slots_of(plan, exp, columns, groups, rows):
+    tokens = plan.shape[1]
+    routes = plan[: plan.shape[0] // 2]
+    halves = columns // EXP_COL
+    hits = [
+        routes == ((c * groups + exp) // halves).astype(jnp.float32) for c in range(columns)
+    ]
+    named = jnp.concatenate(
+        [jnp.max(hit.astype(jnp.float32), axis=0, keepdims=True) for hit in hits], axis=0
+    )
+    upto = lax.broadcasted_iota(jnp.int32, (tokens, tokens), 0) <= lax.broadcasted_iota(
+        jnp.int32, (tokens, tokens), 1
+    )
+    rank = jnp.dot(
+        named.astype(jnp.bfloat16), upto.astype(jnp.bfloat16), preferred_element_type=jnp.float32
+    )
+    rank = jnp.where(named > 0.0, rank - 1.0, -1.0).astype(jnp.int32)
+    slot = lax.broadcasted_iota(jnp.int32, (rows, tokens), 0)
+    return hits, [slot == rank[c : c + 1] for c in range(columns)]
+
+
 def front_kernel(
-    line, columns, att_ref, w_ref, res_ref, gain_ref, sel_ref, stream_ref, all_ref, arr_ref,
-    part, column, rin, rout, total, pack, isend, irecv, osend, orecv, asend, arecv, ysend, yrecv,
+    line, columns, att_ref, w_ref, res_ref, gain_ref, mine_ref, stream_ref, all_ref, arr_ref,
+    plan_ref, part, column, rin, rout, total, pack, isend, irecv, osend, orecv, asend, arecv, ysend, yrecv,
+    psend, precv,
 ):
     long, short = line
     groups = long * short
@@ -300,7 +329,21 @@
     me = lax.axis_index("req")
     place = (exp // short, exp % short)
     outer, inner = place
-    greet(place, line, groups, columns)
+    greet(place, line, groups, columns, True)
+
+    def plan_copy(k):
+        return pltpu.make_async_remote_copy(
+            src_ref=mine_ref,
+            dst_ref=plan_ref.at[outer, inner],
+            send_sem=psend.at[k],
+            recv_sem=precv.at[k],
+            device_id={"exp": (exp + k) % groups},
+            device_id_type=MESH,
+        )
+
+    for k in range(1, groups):
+        plan_copy(k).start()
+    plan_ref[outer, inner] = mine_ref[...]
 
     def fill(o):
         for i in range(short):
@@ -311,6 +354,8 @@
     finish = reduce_scatter(
         place, line, part, fill, column, rin, rout, total, (isend, irecv, osend, orecv)
     )
+    for k in range(1, groups):
+        plan_copy(k).wait_recv()
     stream = (res_ref[...].astype(jnp.float32) + total[...]).astype(jnp.bfloat16)
     stream_ref[...] = stream
     wide = stream.astype(jnp.float32)
@@ -335,7 +380,7 @@
         target = (me + k) % columns
         return pltpu.make_async_remote_copy(
             src_ref=pack.at[o, i, target],
-            dst_ref=arr_ref.at[me, o, i],
+            dst_ref=arr_ref.at[o, me, i],
             send_sem=ysend.at[k, o, i],
             recv_sem=yrecv.at[k, o, i],
             device_id={"req": target},
@@ -343,13 +388,15 @@
         )
 
     def dispatch(o, i):
+        taken = slots_of(plan_ref[o, i], exp, columns, groups, pack.shape[3])[1]
+        select = jnp.concatenate([each.astype(jnp.float32) for each in taken], axis=0)
         rows = jnp.dot(
-            sel_ref[o, i], all_ref[o, i], preferred_element_type=jnp.float32
+            select.astype(jnp.bfloat16), all_ref[o, i], preferred_element_type=jnp.float32
         ).astype(jnp.bfloat16)
         pack[o, i] = rows.reshape(pack.shape[2:])
         for k in range(1, columns):
             to_column(k, o, i).start()
-        arr_ref[me, o, i] = pack[o, i, me]
+        arr_ref[o, me, i] = pack[o, i, me]
 
     def spread(o, distance, side):
         if distance > 0:
@@ -387,6 +434,8 @@
             near(place, long, step - 1, across)
 
     finish()
+    for k in range(1, groups):
+        plan_copy(k).wait_send()
     for o in range(long):
         for i in range(short):
             at_line = inner == i
@@ -424,11 +473,10 @@
             body(outer - distance, distance, 1)
 
 
-def front(attended, out_weight, residual, norm_gain, select, line, columns):
+def front(attended, out_weight, residual, norm_gain, plan, rows, line, columns):
     long, short = line
     tokens, width = residual.shape
     depth = out_weight.shape[0]
-    rows = select.shape[2] // columns
     dma = pltpu.SemaphoreType.DMA
     block = (long, short, tokens, width)
     vmem = pl.BlockSpec(memory_space=pltpu.VMEM)
@@ -438,10 +486,11 @@
         out_shape=(
             jax.ShapeDtypeStruct((tokens, width), bf16),
             jax.ShapeDtypeStruct(block, bf16),
-            jax.ShapeDtypeStruct((columns, long, short, rows, width), bf16),
+            jax.ShapeDtypeStruct((long, columns, short, rows, width), bf16),
+            jax.ShapeDtypeStruct((long, short) + plan.shape, jnp.float32),
         ),
         in_specs=[vmem] * 5,
-        out_specs=(vmem, vmem, vmem),
+        out_specs=(vmem, vmem, vmem, vmem),
         scratch_shapes=[
             pltpu.VMEM(block, bf16),
             pltpu.VMEM((long, tokens, width), bf16),
@@ -457,6 +506,8 @@
             dma((long, short)),
             dma((columns, long, short)),
             dma((columns, long, short)),
+            dma((long * short,)),
+            dma((long * short,)),
         ],
         compiler_params=pltpu.CompilerParams(
             collective_id=0, has_side_effects=True, vmem_limit_bytes=56 * 2**20
@@ -466,53 +517,292 @@
         ),
     )(
         attended.reshape(long, short, tokens, depth), out_weight, residual,
-        norm_gain.reshape(1, width), select,
-    )
+        norm_gain.reshape(1, width), plan,
+    )
+
+
+def order_of(k, place, long):
+    outer = place[0]
+    low = jnp.where(2 * outer <= long - 1, outer, long - 1 - outer)
+    skip = long - 1 - 2 * low
+    pair = jnp.maximum(k - skip, 0)
+    gap = low - pair // 2
+    o = jnp.where(k < skip, long - 1 - k, low + gap * (1 - 2 * (pair % 2)))
+    return jnp.where(2 * outer <= long - 1, o, long - 1 - o)
+
+
+def tiles(width, step):
+    return [(lower, min(lower + step, width)) for lower in range(0, width, step)]
 
 
 def back_kernel(
-    line, part_ref, stream_ref, out_ref, column, rin, rout, total, isend, irecv, osend, orecv
+    line, columns, arr_ref, all_ref, eg_ref, ed_ref, sg_ref, sd_ref, gate_ref, plan_ref,
+    stream_ref, out_ref, rows, part, eg, ed, sg, sd, ret, rin, rout, column, total, hidden,
+    shidden, load, isend, irecv, osend, orecv, ysend, yrecv,
 ):
+    long, short = line
     exp = lax.axis_index("exp")
-    place = (exp // line[1], exp % line[1])
-    greet(place, line, line[0] * line[1], 1)
-    finish = reduce_scatter(
-        place, line, part_ref, lambda o: None, column, rin, rout, total,
-        (isend, irecv, osend, orecv),
-    )
-    out_ref[...] = (stream_ref[...].astype(jnp.float32) + total[...]).astype(jnp.bfloat16)
-    finish()
-
-
-def back(partials, stream, line):
+    me = lax.axis_index("req")
+    place = (exp // short, exp % short)
+    outer, inner = place
+    width = eg.shape[1]
+    bf16, f32 = (jnp.bfloat16, jnp.float32)
+
+    load_rows = pltpu.make_async_copy(arr_ref, rows, load.at[0])
+    load_eg = pltpu.make_async_copy(eg_ref.at[0], eg, load.at[1])
+    load_ed = pltpu.make_async_copy(ed_ref.at[0], ed, load.at[2])
+    load_sg = pltpu.make_async_copy(sg_ref, sg, load.at[3])
+    load_sd = pltpu.make_async_copy(sd_ref, sd, load.at[4])
+    load_all = pltpu.make_async_copy(all_ref, part, load.at[5])
+    for copy in (load_rows, load_eg, load_ed, load_sg, load_sd, load_all):
+        copy.start()
+    greet(place, line, long * short, columns, False)
+
+    def answer_copy(k, o):
+        target = (me + k) % columns
+        return pltpu.make_async_remote_copy(
+            src_ref=rows.at[o, target],
+            dst_ref=ret.at[o, me],
+            send_sem=ysend.at[k, o],
+            recv_sem=yrecv.at[k, o],
+            device_id={"req": target},
+            device_id_type=MESH,
+        )
+
+    load_rows.wait()
+    load_eg.wait()
+    load_ed.wait()
+
+    def expert(k, carry):
+        o = order_of(k, place, long)
+        x = rows[o].reshape(hidden.shape[0], width)
+        for lower, upper in tiles(eg.shape[2], 256):
+            gate = jnp.dot(x, eg[0, :, lower:upper], preferred_element_type=f32)
+            up = jnp.dot(x, eg[1, :, lower:upper], preferred_element_type=f32)
+            hidden[:, lower:upper] = (jax.nn.silu(gate) * up).astype(bf16)
+        for lower, upper in tiles(width, 512):
+            down = jnp.dot(hidden[...], ed[:, lower:upper], preferred_element_type=f32)
+            rows[o, :, :, :, lower:upper] = down.astype(bf16).reshape(
+                rows.shape[1:4] + (upper - lower,)
+            )
+        for j in range(1, columns):
+            answer_copy(j, o).start()
+        ret[o, me] = rows[o, me]
+        return carry
+
+    lax.fori_loop(0, long, expert, 0)
+    load_sg.wait()
+    load_sd.wait()
+    load_all.wait()
+
+    def inner_copy(way, o, i, relay):
+        slot = rin.at[o, i + 1 - way]
+        return pltpu.make_async_remote_copy(
+            src_ref=(slot if relay else part.at[o, i]),
+            dst_ref=slot,
+            send_sem=isend.at[way, o, i],
+            recv_sem=irecv.at[way, o, i],
+            device_id={"exp": outer * short + inner + 1 - 2 * way},
+            device_id_type=MESH,
+        )
+
+    def outer_copy(way, o):
+        return pltpu.make_async_remote_copy(
+            src_ref=column.at[o],
+            dst_ref=rout.at[o + 1 - way],
+            send_sem=osend.at[way, o],
+            recv_sem=orecv.at[way, o],
+            device_id={"exp": (outer + 1 - 2 * way) * short + inner},
+            device_id_type=MESH,
+        )
+
+    def toward(way, gap):
+        i = inner + gap * (1 - 2 * way)
+        ok = (i < short) if way == 0 else (i >= 0)
+        behind = (inner > 0) if way == 0 else (inner < short - 1)
+        return i, ok, behind
+
+    def fill(o):
+        for i in range(short):
+            x = part[o, i]
+            scale = jax.nn.sigmoid(
+                jnp.sum(x.astype(f32) * gate_ref[...].astype(f32), axis=-1, keepdims=True)
+            )
+            for lower, upper in tiles(sg.shape[1], 256):
+                gate = lax.dot_general(
+                    x, sg[0, lower:upper], ROWS_BY_ROWS, preferred_element_type=f32
+                )
+                up = lax.dot_general(
+                    x, sg[1, lower:upper], ROWS_BY_ROWS, preferred_element_type=f32
+                )
+                shidden[:, lower:upper] = (jax.nn.silu(gate) * up).astype(bf16)
+            for lower, upper in tiles(width, 512):
+                down = jnp.dot(shidden[...], sd[:, lower:upper], preferred_element_type=f32)
+                part[o, i, :, lower:upper] = (scale * down).astype(bf16)
+        for j in range(1, columns):
+            answer_copy(j, o).wait_recv()
+        for i in range(short):
+            hits, taken = slots_of(
+                plan_ref[o, i], exp, columns, long * short, rows.shape[3]
+            )
+            weights = plan_ref[o, i, plan_ref.shape[2] // 2 :]
+            spread = jnp.concatenate(
+                [
+                    jnp.where(
+                        taken[c],
+                        jnp.sum(
+                            jnp.where(hits[c], weights, 0.0), axis=0, keepdims=True
+                        ),
+                        0.0,
+                    )
+                    for c in range(columns)
+                ],
+                axis=0,
+            ).astype(bf16)
+            for lower, upper in tiles(width, 512):
+                picked = ret[o, :, i, :, lower:upper].reshape(-1, upper - lower)
+                routed = lax.dot_general(
+                    spread, picked, (((0,), (0,)), ((), ())), preferred_element_type=f32
+                )
+                part[o, i, :, lower:upper] = (
+                    part[o, i, :, lower:upper].astype(f32) + routed
+                ).astype(bf16)
+
+    def first(o):
+        fill(o)
+        for way in (0, 1):
+            for gap in range(short - 1, 0, -1):
+                i, ok, behind = toward(way, gap)
+                if short > 2:
+                    ok = ok & jnp.logical_not(behind)
+
+                @pl.when(ok)
+                def _():
+                    inner_copy(way, o, i, False).start()
+
+    def second(o, own):
+        if short > 2:
+            for way in (0, 1):
+                for gap in range(short - 1, 0, -1):
+                    i, ok, behind = toward(way, gap)
+
+                    @pl.when(ok & behind)
+                    def _():
+                        inner_copy(way, o, i, True).wait_recv()
+                        slot = i + 1 - way
+                        rin[o, slot] = (
+                            rin[o, slot].astype(f32) + part[o, i].astype(f32)
+                        ).astype(bf16)
+                        inner_copy(way, o, i, True).start()
+
+        total[...] = part[o, inner].astype(f32)
+        for way, behind in ((0, inner > 0), (1, inner < short - 1)):
+            @pl.when(behind)
+            def _():
+                inner_copy(way, o, inner, False).wait_recv()
+                total[...] += rin[o, inner + 1 - way].astype(f32)
+
+        for way, behind in ((0, outer > 0), (1, outer < long - 1)):
+            if not own:
+                behind = behind & ((o > outer) if way == 0 else (o < outer))
+
+            @pl.when(behind)
+            def _():
+                outer_copy(way, o).wait_recv()
+                total[...] += rout[o + 1 - way].astype(f32)
+
+        if not own:
+            column[o] = total[...].astype(bf16)
+            for way, ahead in ((0, o > outer), (1, o < outer)):
+                @pl.when(ahead)
+                def _():
+                    outer_copy(way, o).start()
+
+    def combine(k, carry):
+        first(order_of(k, place, long))
+
+        @pl.when(k > 0)
+        def _():
+            second(order_of(k - 1, place, long), False)
+
+        return carry
+
+    lax.fori_loop(0, long, combine, 0)
+    second(outer, True)
+    out_ref[...] = (stream_ref[...].astype(f32) + total[...]).astype(bf16)
+
+    for o in range(long):
+        for i in range(short):
+            @pl.when(inner < i)
+            def _():
+                inner_copy(0, o, i, False).wait_send()
+
+            @pl.when(inner > i)
+            def _():
+                inner_copy(1, o, i, False).wait_send()
+
+        @pl.when(outer < o)
+        def _():
+            outer_copy(0, o).wait_send()
+
+        @pl.when(outer > o)
+        def _():
+            outer_copy(1, o).wait_send()
+
+        for j in range(1, columns):
+            answer_copy(j, o).wait_send()
+
+
+def back(
+    arrived, gathered, expert_gate_up, expert_down, shared_gate_up, shared_down, shared_gate,
+    plan, stream, line, columns,
+):
     long, short = line
     tokens, width = stream.shape
+    count = arrived.shape[3]
+    hid, shid = (expert_down.shape[1], shared_down.shape[0])
     dma = pltpu.SemaphoreType.DMA
     block = (long, short, tokens, width)
     vmem = pl.BlockSpec(memory_space=pltpu.VMEM)
+    hbm = pl.BlockSpec(memory_space=pl.ANY)
     bf16 = jnp.bfloat16
     return pl.pallas_call(
-        functools.partial(back_kernel, line),
+        functools.partial(back_kernel, line, columns),
         out_shape=jax.ShapeDtypeStruct((tokens, width), bf16),
-        in_specs=[vmem] * 2,
+        in_specs=[hbm] * 6 + [vmem] * 3,
         out_specs=vmem,
         scratch_shapes=[
+            pltpu.VMEM(arrived.shape, bf16),
+            pltpu.VMEM(block, bf16),
+            pltpu.VMEM(expert_gate_up.shape[1:], bf16),
+            pltpu.VMEM(expert_down.shape[1:], bf16),
+            pltpu.VMEM(shared_gate_up.shape, bf16),
+            pltpu.VMEM(shared_down.shape, bf16),
+            pltpu.VMEM(arrived.shape, bf16),
+            pltpu.VMEM((long, short + 1, tokens, width), bf16),
+            pltpu.VMEM((long + 1, tokens, width), bf16),
             pltpu.VMEM((long, tokens, width), bf16),
-            pltpu.VMEM((2,) + block, bf16),
-            pltpu.VMEM((2, long, tokens, width), bf16),
             pltpu.VMEM((tokens, width), jnp.float32),
+            pltpu.VMEM((columns * short * count, hid), bf16),
+            pltpu.VMEM((tokens, shid), bf16),
+            dma((6,)),
             dma((2, long, short)),
             dma((2, long, short)),
             dma((2, long)),
             dma((2, long)),
+            dma((columns, long)),
+            dma((columns, long)),
         ],
         compiler_params=pltpu.CompilerParams(
-            collective_id=1, has_side_effects=True, vmem_limit_bytes=56 * 2**20
+            collective_id=1, has_side_effects=True, vmem_limit_bytes=60 * 2**20
         ),
         cost_estimate=pl.CostEstimate(
-            flops=10**7, bytes_accessed=2 * 10**7, transcendentals=0
+            flops=3 * 10**10, bytes_accessed=5 * 10**7, transcendentals=0
         ),
-    )(partials.reshape(block), stream)
+    )(
+        arrived, gathered, expert_gate_up, expert_down, shared_gate_up, shared_down,
+        shared_gate.reshape(1, width), plan, stream,
+    )
 
 
 def on_device(
@@ -535,66 +825,21 @@
     attended = attend(prefill_qkv, decode_qkv, cache_pool, page_table, cache_len)
     groups = lax.axis_size("exp")
     columns = lax.axis_size("req")
-    tok_rows = residual.shape[0]
-    model_width = out_weight.shape[1]
     line = (LINE, groups // LINE)
-    rank_of, weight_of = dispatch_plan(routes, route_weight)
+    plan = jnp.concatenate([routes.T.astype(jnp.float32), route_weight.T], axis=0)
     rows = row_limit(routes.shape, groups)
-    select = (
-        (jnp.arange(rows, dtype=jnp.int32)[None, None, :, None] == rank_of[:, :, None, :])
-        .astype(jnp.bfloat16)
-        .reshape(line + (columns * rows, tok_rows))
-    )
-    stream, gathered, arrived = front(
-        attended, out_weight, residual, norm_gain, select, line, columns
-    )
-    block_rows = gathered.reshape(groups * tok_rows, model_width)
-    arrived = arrived.reshape(columns * groups * rows, model_width)
-
-    gate_part = jnp.dot(block_rows, shared_gate_up[0], preferred_element_type=jnp.float32)
-    up_part = jnp.dot(block_rows, shared_gate_up[1], preferred_element_type=jnp.float32)
-    hidden = (jax.nn.silu(gate_part) * up_part).astype(jnp.bfloat16)
-    shared_scale = jax.nn.sigmoid(
-        jnp.dot(block_rows, shared_gate, preferred_element_type=jnp.float32)
-    )
-    shared = jnp.dot(hidden, shared_down, preferred_element_type=jnp.float32)
-    shared = shared_scale[:, None] * shared
-
-    expert_gate = jnp.dot(arrived, expert_gate_up[0, 0], preferred_element_type=jnp.float32)
-    expert_up = jnp.dot(arrived, expert_gate_up[0, 1], preferred_element_type=jnp.float32)
-    hidden = (jax.nn.silu(expert_gate) * expert_up).astype(jnp.bfloat16)
-    answer = jnp.dot(hidden, expert_down[0], preferred_element_type=jnp.float32).astype(
-        jnp.bfloat16
-    )
-    returned = lax.all_to_all(answer, "req", split_axis=0, concat_axis=0, tiled=True)
-    returned = returned.reshape(columns, groups, rows, model_width)
-    spread = jnp.where(
-        jnp.arange(rows, dtype=jnp.int32)[None, None, :, None] == rank_of[:, :, None, :],
-        weight_of[:, :, None, :],
-        0.0,
-    ).astype(jnp.bfloat16)
-    routed = jnp.einsum("gcrt,cgrd->gtd", spread, returned, preferred_element_type=jnp.float32)
-    partials = (shared.reshape(routed.shape) + routed).astype(jnp.bfloat16)
-    return back(partials, stream, line)
+    stream, gathered, arrived, plan = front(
+        attended, out_weight, residual, norm_gain, plan, rows, line, columns
+    )
+    return back(
+        arrived, gathered, expert_gate_up, expert_down, jnp.swapaxes(shared_gate_up, 1, 2),
+        shared_down, shared_gate, plan, stream, line, columns,
+    )
 
 
 def row_limit(routes_shape, groups):
     tok_rows, route_count = routes_shape
     return max(2, tok_rows * route_count * 2 // (EXP_COL * groups))
-
-
-def dispatch_plan(routes, route_weight):
-    groups = lax.axis_size("exp")
-    columns = lax.axis_size("req")
-    halves = columns // EXP_COL
-    all_routes = lax.all_gather(routes.T, "exp", axis=0)
-    all_weights = lax.all_gather(route_weight.T, "exp", axis=0)
-    mine = (jnp.arange(columns, dtype=jnp.int32) * groups + lax.axis_index("exp")) // halves
-    onehot = all_routes[:, None] == mine[None, :, None, None]
-    named = jnp.any(onehot, axis=2).astype(jnp.int32)
-    rank_of = jnp.where(named > 0, jnp.cumsum(named, axis=2) - 1, -1)
-    weight_of = jnp.sum(jnp.where(onehot, all_weights[:, None], 0.0), axis=2)
-    return rank_of, weight_of
 
 
 def solution(mesh):

time: 339 us -> 237 us (0.70)
  the two profiles are of different devices: /device:TPU:0 before, /device:TPU:3 now
where the time goes in v2:
time: 237 us; the launch traced here: 233 us
  Pallas kernels  224 us (95%)
  local copies, waits for them, and re-layouts  5.68 us (2%)
  other arithmetic  3.42 us (1%)
    pallas_call x1, Pallas kernels, front(): pl.pallas_call(functools.partial(front_kernel, line, columns), out_shape=...  116 us
    pallas_call x1, Pallas kernels, back(): pl.pallas_call(functools.partial(back_kernel, line, columns), out_shape=j...  95.3 us
    pallas_call x1, Pallas kernels, attend(): pl.pallas_call(functools.partial(attention_kernel, heads), grid=(steps,),...  12.2 us

profile of v2, /device:TPU:3, one launch (start us, length us, event | category | flops | bytes accessed | tf_op | source)
XLA Modules:
  0.0 232.8 jit_solution(8734411963105267677)
XLA Ops:
  0.0 0.7 broadcast_subtract_fusion
  0.7 0.7 broadcast_compare_fusion
  1.5 1.3 select_reduce_fusion.1
  2.7 0.1 select_bitcast_fusion
  2.8 0.1 copy.18
  2.9 0.7 slice_bitcast_fusion
  3.6 0.0 copy-start
  3.6 1.4 copy-done
  5.1 0.0 copy-start.2
  5.1 0.0 copy-start.3
  5.1 12.2 %shard_map.145 = bf16[1040,256]{1,0:T(8,128)(2,1)S(1)} custom-call(bf16[2,3,512,256]{3,2,1,0:T(8,128)(2,1)S(1)} %copy-done, bf16[2,3,512,256]{3,2,1,0:T(8,128)(2,1)S(1)} %copy-done, bf16[2,3,512,256]{3,2,1,0:T(8,128)(2,1)S(1)} %copy-done, bf16[16,256]{1,0:T(8,128)(2,1)S(1)} %get-tuple-element.16.dq_ref, bf16[16,256]{1,0:T(8,128)(2,1)S(1)} %get-tuple-element.17.dk_ref, ...), custom_call_target="tpu_custom_call" | custom-call | flops 2000000000 | bytes 17825792 | tf_op jit(solution)/shard_map/pallas_call | solution.py:118
  17.2 0.9 reshape.108.att_ref
  18.2 0.0 copy-done.2
  18.2 0.0 copy-done.3
  18.2 0.6 pad_maximum_fusion.mine_ref
  18.8 0.0 copy-start.1
  18.8 116.2 %shard_map.146 = (bf16[130,2048]{1,0:T(8,128)(2,1)}, bf16[4,2,130,2048]{3,2,1,0:T(8,128)(2,1)}, bf16[4,4,2,32,2048]{4,3,2,1,0:T(8,128)(2,1)}, f32[4,2,8,130]{3,2,1,0:T(8,128)}) custom-call(bf16[4,2,130,256]{3,2,1,0:T(8,128)(2,1)} %reshape.108.att_ref, bf16[256,2048]{1,0:T(8,128)(2,1)} %w_ref.1, bf16[130,2048]{1,0:T(8,128)(2,1)} %res_ref.1, ...), custom_call_target="tpu_custom_call" | custom-call | flops 4000000000 | bytes 20000000 | tf_op jit(solution)/shard_map/pallas_call | solution.py:484
  135.0 0.0 copy-done.1
  135.0 0.6 reshape.110.gate_ref
  135.6 95.3 %shard_map.147 = bf16[130,2048]{1,0:T(8,128)(2,1)} custom-call(bf16[4,4,2,32,2048]{4,3,2,1,0:T(8,128)(2,1)} %get-tuple-element.9.arr_ref, bf16[4,2,130,2048]{3,2,1,0:T(8,128)(2,1)} %get-tuple-element.10.all_ref, bf16[1,2,2048,1408]{3,2,1,0:T(8,128)(2,1)} %eg_ref.1, bf16[1,1408,2048]{2,1,0:T(8,128)(2,1)} %ed_ref.1, bf16[2,704,2048]{2,1,0:T(8,128)(2,1)} %bitcast.22, ...), custom_call_target="tpu_custom_call" | custom-call | flops 30000001024 | bytes 50000000 | tf_op jit(solution)/shard_map/pallas_call | solution.py:769
  230.9 1.9 copy.20
  (2 shorter events, 0.0 us)
Async XLA Ops:
  3.6 1.4 copy-start
  5.1 13.1 %copy-start.2 = (s32[130,4]{0,1:T(4,128)S(1)}, s32[130,4]{0,1:T(4,128)}, u32[]{:S(2)}) copy-start(s32[130,4]{0,1:T(4,128)} %param.26) | copy-start | bytes 6244
  5.1 13.1 %copy-start.3 = (f32[130,4]{0,1:T(4,128)S(1)}, f32[130,4]{0,1:T(4,128)}, u32[]{:S(2)}) copy-start(f32[130,4]{0,1:T(4,128)} %param.27) | copy-start | bytes 6244
  18.8 116.2 %copy-start.1 = (bf16[2048]{0:T(1024)(128)(2,1)S(1)}, bf16[2048]{0:T(1024)(128)(2,1)}, u32[]{:S(2)}) copy-start(bf16[2048]{0:T(1024)(128)(2,1)} %param.25) | copy-start | bytes 12292

commit v3 on v2

--- a/solution.py
+++ b/solution.py
@@ -180,123 +180,6 @@
     pl.semaphore_wait(barrier, count)
 
 
-def visit(place, long, farthest_first, body):
-    outer = place[0]
-    distances = range(long - 1, -1, -1) if farthest_first else range(long)
-    for distance in distances:
-        @pl.when(outer + distance < long)
-        def _():
-            body(outer + distance, distance, 0)
-
-        if distance > 0:
-            @pl.when(outer - distance >= 0)
-            def _():
-                body(outer - distance, distance, 1)
-
-
-def reduce_scatter(place, line, part, fill, column, rin, rout, total, sems):
-    outer, inner = place
-    long, short = line
-    isend, irecv, osend, orecv = sems
-
-    def inner_copy(way, o, i, relay):
-        target = outer * short + inner + (1 if way == 0 else -1)
-        return pltpu.make_async_remote_copy(
-            src_ref=(rin.at[way, o, i] if relay else part.at[o, i]),
-            dst_ref=rin.at[way, o, i],
-            send_sem=isend.at[way, o, i],
-            recv_sem=irecv.at[way, o, i],
-            device_id={"exp": target},
-            device_id_type=MESH,
-        )
-
-    def outer_copy(way, o):
-        target = (outer + (1 if way == 0 else -1)) * short + inner
-        return pltpu.make_async_remote_copy(
-            src_ref=column.at[o],
-            dst_ref=rout.at[way, o],
-            send_sem=osend.at[way, o],
-            recv_sem=orecv.at[way, o],
-            device_id={"exp": target},
-            device_id_type=MESH,
-        )
-
-    def first(o, distance, side):
-        fill(o)
-        for way in (0, 1):
-            for gap in range(short - 1, 0, -1):
-                i = inner + gap if way == 0 else inner - gap
-                ok = (i < short) if way == 0 else (i >= 0)
-                behind = (inner > 0) if way == 0 else (inner < short - 1)
-                if short == 2:
-                    @pl.when(ok)
-                    def _():
-                        inner_copy(way, o, i, False).start()
-                else:
-                    @pl.when(ok & jnp.logical_not(behind))
-                    def _():
-                        inner_copy(way, o, i, False).start()
-
-    visit(place, long, True, first)
-
-    def second(o, distance, side):
-        if short > 2:
-            for way in (0, 1):
-                for gap in range(short - 1, 0, -1):
-                    i = inner + gap if way == 0 else inner - gap
-                    ok = (i < short) if way == 0 else (i >= 0)
-                    behind = (inner > 0) if way == 0 else (inner < short - 1)
-
-                    @pl.when(ok & behind)
-                    def _():
-                        inner_copy(way, o, i, True).wait_recv()
-                        rin[way, o, i] = (
-                            rin[way, o, i].astype(jnp.float32) + part[o, i].astype(jnp.float32)
-                        ).astype(jnp.bfloat16)
-                        inner_copy(way, o, i, True).start()
-
-        total[...] = part[o, inner].astype(jnp.float32)
-        for way, behind in ((0, inner > 0), (1, inner < short - 1)):
-            @pl.when(behind)
-            def _():
-                inner_copy(way, o, inner, False).wait_recv()
-                total[...] += rin[way, o, inner].astype(jnp.float32)
-
-        for way, behind in ((0, outer > 0), (1, outer < long - 1)):
-            if distance == 0 or way == side:
-                @pl.when(behind)
-                def _():
-                    outer_copy(way, o).wait_recv()
-                    total[...] += rout[way, o].astype(jnp.float32)
-
-        if distance > 0:
-            column[o] = total[...].astype(jnp.bfloat16)
-            outer_copy(side, o).start()
-
-    visit(place, long, True, second)
-
-    def finish():
-        for o in range(long):
-            for i in range(short):
-                @pl.when(inner < i)
-                def _():
-                    inner_copy(0, o, i, False).wait_send()
-
-                @pl.when(inner > i)
-                def _():
-                    inner_copy(1, o, i, False).wait_send()
-
-            @pl.when(outer < o)
-            def _():
-                outer_copy(0, o).wait_send()
-
-            @pl.when(outer > o)
-            def _():
-                outer_copy(1, o).wait_send()
-
-    return finish
-
-
 def slots_of(plan, exp, columns, groups, rows):
     tokens = plan.shape[1]
     routes = plan[: plan.shape[0] // 2]
@@ -319,9 +202,9 @@
 
 
 def front_kernel(
-    line, columns, att_ref, w_ref, res_ref, gain_ref, mine_ref, stream_ref, all_ref, arr_ref,
-    plan_ref, part, column, rin, rout, total, pack, isend, irecv, osend, orecv, asend, arecv, ysend, yrecv,
-    psend, precv,
+    line, columns, att_ref, w_refs, res_ref, gain_ref, mine_ref, stream_ref, all_ref, arr_ref,
+    plan_ref, attin, column, rout, total, pack, isend, irecv, osend, orecv, asend, arecv, bsend,
+    brecv, ysend, yrecv, psend, precv,
 ):
     long, short = line
     groups = long * short
@@ -329,7 +212,30 @@
     me = lax.axis_index("req")
     place = (exp // short, exp % short)
     outer, inner = place
+    f32, bf16 = (jnp.float32, jnp.bfloat16)
+    direct = all_ref.shape[3] // 8 // 128 * 128 if short == 2 else 0
     greet(place, line, groups, columns, True)
+
+    def rows_copy(k, o):
+        target = (inner + k) % short
+        return pltpu.make_async_remote_copy(
+            src_ref=att_ref.at[o, target],
+            dst_ref=attin.at[k, o],
+            send_sem=isend.at[k, o],
+            recv_sem=irecv.at[k, o],
+            device_id={"exp": outer * short + target},
+            device_id_type=MESH,
+        )
+
+    def outer_copy(way, o):
+        return pltpu.make_async_remote_copy(
+            src_ref=column.at[o],
+            dst_ref=rout.at[o + 1 - way],
+            send_sem=osend.at[way, o],
+            recv_sem=orecv.at[way, o],
+            device_id={"exp": (outer + 1 - 2 * way) * short + inner},
+            device_id_type=MESH,
+        )
 
     def plan_copy(k):
         return pltpu.make_async_remote_copy(
@@ -341,37 +247,65 @@
             device_id_type=MESH,
         )
 
+    def send_rows(n, carry):
+        for k in range(1, short):
+            rows_copy(k, order_of(n, place, long)).start()
+        return carry
+
+    lax.fori_loop(0, long, send_rows, 0)
     for k in range(1, groups):
         plan_copy(k).start()
     plan_ref[outer, inner] = mine_ref[...]
 
-    def fill(o):
-        for i in range(short):
-            part[o, i] = jnp.dot(
-                att_ref[o, i], w_ref[...], preferred_element_type=jnp.float32
-            ).astype(jnp.bfloat16)
-
-    finish = reduce_scatter(
-        place, line, part, fill, column, rin, rout, total, (isend, irecv, osend, orecv)
-    )
+    def project(o, own):
+        total[...] = jnp.dot(att_ref[o, inner], w_refs[0][...], preferred_element_type=f32)
+        for k in range(1, short):
+            rows_copy(k, o).wait_recv()
+            total[...] += jnp.dot(attin[k, o], w_refs[k][...], preferred_element_type=f32)
+        for way, behind in ((0, outer > 0), (1, outer < long - 1)):
+            if not own:
+                behind = behind & ((o > outer) if way == 0 else (o < outer))
+
+            @pl.when(behind)
+            def _():
+                outer_copy(way, o).wait_recv()
+                total[...] += rout[o + 1 - way].astype(f32)
+
+        if not own:
+            column[o] = total[...].astype(bf16)
+            for way, ahead in ((0, o > outer), (1, o < outer)):
+                @pl.when(ahead)
+                def _():
+                    outer_copy(way, o).start()
+
+    def project_far(n, carry):
+        project(order_of(n, place, long), False)
+        return carry
+
+    lax.fori_loop(0, long - 1, project_far, 0)
+    project(outer, True)
     for k in range(1, groups):
         plan_copy(k).wait_recv()
-    stream = (res_ref[...].astype(jnp.float32) + total[...]).astype(jnp.bfloat16)
+    stream = (res_ref[...].astype(f32) + total[...]).astype(bf16)
     stream_ref[...] = stream
-    wide = stream.astype(jnp.float32)
+    wide = stream.astype(f32)
     all_ref[outer, inner] = (
         wide
         * lax.rsqrt(jnp.mean(wide * wide, axis=-1, keepdims=True) + 1e-06)
         * gain_ref[...]
-    ).astype(jnp.bfloat16)
-
-    def pass_on(way, o, i):
+    ).astype(bf16)
+
+    def pass_on(way, o, i, lanes="all"):
         target = exp + (short, -short, 1, -1)[way]
+        width = all_ref.shape[3]
+        lower, upper = {"all": (0, width), "last": (0, width - direct), "direct": (width - direct, width)}[lanes]
+        view = all_ref.at[o, i] if lanes == "all" else all_ref.at[o, i, :, lower:upper]
+        sems = (bsend, brecv) if lanes == "direct" else (asend, arecv)
         return pltpu.make_async_remote_copy(
-            src_ref=all_ref.at[o, i],
-            dst_ref=all_ref.at[o, i],
-            send_sem=asend.at[way, o, i],
-            recv_sem=arecv.at[o, i],
+            src_ref=view,
+            dst_ref=view,
+            send_sem=sems[0].at[way, o, i],
+            recv_sem=sems[1].at[o, i],
             device_id={"exp": target},
             device_id_type=MESH,
         )
@@ -389,27 +323,30 @@
 
     def dispatch(o, i):
         taken = slots_of(plan_ref[o, i], exp, columns, groups, pack.shape[3])[1]
-        select = jnp.concatenate([each.astype(jnp.float32) for each in taken], axis=0)
+        select = jnp.concatenate([each.astype(f32) for each in taken], axis=0)
         rows = jnp.dot(
-            select.astype(jnp.bfloat16), all_ref[o, i], preferred_element_type=jnp.float32
-        ).astype(jnp.bfloat16)
+            select.astype(bf16), all_ref[o, i], preferred_element_type=f32
+        ).astype(bf16)
         pack[o, i] = rows.reshape(pack.shape[2:])
         for k in range(1, columns):
             to_column(k, o, i).start()
         arr_ref[o, me, i] = pack[o, i, me]
 
-    def spread(o, distance, side):
-        if distance > 0:
-            pass_on(0, o, inner).wait_recv()
+    def onward(o, i, distance, side, lanes):
         for way, ahead in ((0, outer < long - 1), (1, outer > 0)):
             if distance == 0 or way == 1 - side:
                 @pl.when(ahead)
                 def _():
-                    pass_on(way, o, inner).start()
+                    pass_on(way, o, i, lanes).start()
+
+    def spread(o, distance, side):
+        if distance > 0:
+            pass_on(0, o, inner).wait_recv()
+        onward(o, inner, distance, side, "all")
         for way, ahead in ((2, inner < short - 1), (3, inner > 0)):
             @pl.when(ahead)
             def _():
-                pass_on(way, o, inner).start()
+                pass_on(way, o, inner, "last" if direct and distance else "all").start()
         dispatch(o, inner)
 
     def across(o, distance, side):
@@ -420,7 +357,14 @@
             ):
                 @pl.when(ok)
                 def _():
-                    pass_on(way, o, i).wait_recv()
+                    if direct and distance:
+                        pass_on(0, o, i, "direct").wait_recv()
+                        onward(o, i, distance, side, "direct")
+                        pass_on(way, o, i, "last").wait_recv()
+                    else:
+                        pass_on(way, o, i).wait_recv()
+                        if direct:
+                            onward(o, i, distance, side, "direct")
                     if short > 2:
                         @pl.when(ahead)
                         def _():
@@ -433,27 +377,46 @@
         if step > 0:
             near(place, long, step - 1, across)
 
-    finish()
     for k in range(1, groups):
         plan_copy(k).wait_send()
     for o in range(long):
+        for k in range(1, short):
+            rows_copy(k, o).wait_send()
+
+        @pl.when(outer < o)
+        def _():
+            outer_copy(0, o).wait_send()
+
+        @pl.when(outer > o)
+        def _():
+            outer_copy(1, o).wait_send()
+
         for i in range(short):
-            at_line = inner == i
-            @pl.when(at_line & (outer >= o) & (outer < long - 1))
-            def _():
-                pass_on(0, o, i).wait_send()
-
-            @pl.when(at_line & (outer <= o) & (outer > 0))
-            def _():
-                pass_on(1, o, i).wait_send()
-
-            @pl.when((inner >= i) & (inner < short - 1))
-            def _():
-                pass_on(2, o, i).wait_send()
-
-            @pl.when((inner <= i) & (inner > 0))
-            def _():
-                pass_on(3, o, i).wait_send()
+            for lanes, there in (("all", inner == i), ("direct", inner != i)):
+                if lanes == "all" or direct:
+                    @pl.when(there & (outer >= o) & (outer < long - 1))
+                    def _():
+                        pass_on(0, o, i, lanes).wait_send()
+
+                    @pl.when(there & (outer <= o) & (outer > 0))
+                    def _():
+                        pass_on(1, o, i, lanes).wait_send()
+
+            for way, sent in (
+                (2, (inner >= i) & (inner < short - 1)), (3, (inner <= i) & (inner > 0)),
+            ):
+                if direct:
+                    @pl.when(sent & (inner == i) & (outer == o))
+                    def _():
+                        pass_on(way, o, i).wait_send()
+
+                    @pl.when(sent & (inner == i) & (outer != o))
+                    def _():
+                        pass_on(way, o, i, "last").wait_send()
+                else:
+                    @pl.when(sent)
+                    def _():
+                        pass_on(way, o, i).wait_send()
 
             for k in range(1, columns):
                 to_column(k, o, i).wait_send()
@@ -473,35 +436,40 @@
             body(outer - distance, distance, 1)
 
 
-def front(attended, out_weight, residual, norm_gain, plan, rows, line, columns):
+def front(attended, out_weights, residual, norm_gain, plan, rows, line, columns):
     long, short = line
     tokens, width = residual.shape
-    depth = out_weight.shape[0]
+    depth = out_weights[0].shape[0]
     dma = pltpu.SemaphoreType.DMA
     block = (long, short, tokens, width)
     vmem = pl.BlockSpec(memory_space=pltpu.VMEM)
     bf16 = jnp.bfloat16
+
+    def kernel(att_ref, *refs):
+        front_kernel(line, columns, att_ref, refs[:short], *refs[short:])
+
     return pl.pallas_call(
-        functools.partial(front_kernel, line, columns),
+        kernel,
         out_shape=(
             jax.ShapeDtypeStruct((tokens, width), bf16),
             jax.ShapeDtypeStruct(block, bf16),
             jax.ShapeDtypeStruct((long, columns, short, rows, width), bf16),
             jax.ShapeDtypeStruct((long, short) + plan.shape, jnp.float32),
         ),
-        in_specs=[vmem] * 5,
+        in_specs=[vmem] * (4 + short),
         out_specs=(vmem, vmem, vmem, vmem),
         scratch_shapes=[
-            pltpu.VMEM(block, bf16),
+            pltpu.VMEM((short, long, tokens, depth), bf16),
             pltpu.VMEM((long, tokens, width), bf16),
-            pltpu.VMEM((2,) + block, bf16),
-            pltpu.VMEM((2, long, tokens, width), bf16),
+            pltpu.VMEM((long + 1, tokens, width), bf16),
             pltpu.VMEM((tokens, width), jnp.float32),
             pltpu.VMEM((long, short, columns, rows, width), bf16),
-            dma((2, long, short)),
-            dma((2, long, short)),
+            dma((short, long)),
+            dma((short, long)),
             dma((2, long)),
             dma((2, long)),
+            dma((4, long, short)),
+            dma((long, short)),
             dma((4, long, short)),
             dma((long, short)),
             dma((columns, long, short)),
@@ -516,7 +484,7 @@
             flops=4 * 10**9, bytes_accessed=2 * 10**7, transcendentals=0
         ),
     )(
-        attended.reshape(long, short, tokens, depth), out_weight, residual,
+        attended.reshape(long, short, tokens, depth), *out_weights, residual,
         norm_gain.reshape(1, width), plan,
     )
 
@@ -538,7 +506,8 @@
 def back_kernel(
     line, columns, arr_ref, all_ref, eg_ref, ed_ref, sg_ref, sd_ref, gate_ref, plan_ref,
     stream_ref, out_ref, rows, part, eg, ed, sg, sd, ret, rin, rout, column, total, hidden,
-    shidden, load, isend, irecv, osend, orecv, ysend, yrecv,
+    shidden, sideout, sidecol, sidein, load, isend, irecv, osend, orecv, ysend, yrecv, ssend,
+    srecv, tsend, trecv,
 ):
     long, short = line
     exp = lax.axis_index("exp")
@@ -546,6 +515,9 @@
     place = (exp // short, exp % short)
     outer, inner = place
     width = eg.shape[1]
+    direct = sidecol.shape[2] if short == 2 else 0
+    near_lanes = slice(0, width - direct)
+    far_lanes = slice(width - direct, width)
     bf16, f32 = (jnp.bfloat16, jnp.float32)
 
     load_rows = pltpu.make_async_copy(arr_ref, rows, load.at[0])
@@ -554,7 +526,7 @@
     load_sg = pltpu.make_async_copy(sg_ref, sg, load.at[3])
     load_sd = pltpu.make_async_copy(sd_ref, sd, load.at[4])
     load_all = pltpu.make_async_copy(all_ref, part, load.at[5])
-    for copy in (load_rows, load_eg, load_ed, load_sg, load_sd, load_all):
+    for copy in (load_rows, load_eg, load_ed):
         copy.start()
     greet(place, line, long * short, columns, False)
 
@@ -571,15 +543,21 @@
 
     load_rows.wait()
     load_eg.wait()
-    load_ed.wait()
-
-    def expert(k, carry):
+    for copy in (load_all, load_sg, load_sd):
+        copy.start()
+
+    def expert(k):
         o = order_of(k, place, long)
         x = rows[o].reshape(hidden.shape[0], width)
         for lower, upper in tiles(eg.shape[2], 256):
             gate = jnp.dot(x, eg[0, :, lower:upper], preferred_element_type=f32)
             up = jnp.dot(x, eg[1, :, lower:upper], preferred_element_type=f32)
             hidden[:, lower:upper] = (jax.nn.silu(gate) * up).astype(bf16)
+
+        @pl.when(k == 0)
+        def _():
+            load_ed.wait()
+
         for lower, upper in tiles(width, 512):
             down = jnp.dot(hidden[...], ed[:, lower:upper], preferred_element_type=f32)
             rows[o, :, :, :, lower:upper] = down.astype(bf16).reshape(
@@ -588,17 +566,14 @@
         for j in range(1, columns):
             answer_copy(j, o).start()
         ret[o, me] = rows[o, me]
-        return carry
-
-    lax.fori_loop(0, long, expert, 0)
-    load_sg.wait()
-    load_sd.wait()
-    load_all.wait()
 
     def inner_copy(way, o, i, relay):
         slot = rin.at[o, i + 1 - way]
+        source = slot if relay else part.at[o, i]
+        if direct:
+            slot, source = slot.at[:, near_lanes], source.at[:, near_lanes]
         return pltpu.make_async_remote_copy(
-            src_ref=(slot if relay else part.at[o, i]),
+            src_ref=source,
             dst_ref=slot,
             send_sem=isend.at[way, o, i],
             recv_sem=irecv.at[way, o, i],
@@ -615,6 +590,47 @@
             device_id={"exp": (outer + 1 - 2 * way) * short + inner},
             device_id_type=MESH,
         )
+
+    def side_copy(way, o):
+        return pltpu.make_async_remote_copy(
+            src_ref=sidecol.at[o],
+            dst_ref=sideout.at[o + 1 - way],
+            send_sem=ssend.at[way, o],
+            recv_sem=srecv.at[way, o],
+            device_id={"exp": (outer + 1 - 2 * way) * short + inner},
+            device_id_type=MESH,
+        )
+
+    def last_copy():
+        return pltpu.make_async_remote_copy(
+            src_ref=sidecol.at[outer],
+            dst_ref=sidein,
+            send_sem=tsend,
+            recv_sem=trecv,
+            device_id={"exp": outer * short + 1 - inner},
+            device_id_type=MESH,
+        )
+
+    def side(o, own):
+        value = part[o, 1 - inner, :, far_lanes].astype(f32)
+        total[:, far_lanes] = value
+        for way, behind in ((0, outer > 0), (1, outer < long - 1)):
+            if not own:
+                behind = behind & ((o > outer) if way == 0 else (o < outer))
+
+            @pl.when(behind)
+            def _():
+                side_copy(way, o).wait_recv()
+                total[:, far_lanes] += sideout[o + 1 - way].astype(f32)
+
+        sidecol[o] = total[:, far_lanes].astype(bf16)
+        if own:
+            last_copy().start()
+        else:
+            for way, ahead in ((0, o > outer), (1, o < outer)):
+                @pl.when(ahead)
+                def _():
+                    side_copy(way, o).start()
 
     def toward(way, gap):
         i = inner + gap * (1 - 2 * way)
@@ -695,12 +711,14 @@
                         ).astype(bf16)
                         inner_copy(way, o, i, True).start()
 
+        if direct:
+            side(o, own)
         total[...] = part[o, inner].astype(f32)
         for way, behind in ((0, inner > 0), (1, inner < short - 1)):
             @pl.when(behind)
             def _():
                 inner_copy(way, o, inner, False).wait_recv()
-                total[...] += rin[o, inner + 1 - way].astype(f32)
+                total[:, near_lanes] += rin[o, inner + 1 - way, :, near_lanes].astype(f32)
 
         for way, behind in ((0, outer > 0), (1, outer < long - 1)):
             if not own:
@@ -718,17 +736,33 @@
                 def _():
                     outer_copy(way, o).start()
 
-    def combine(k, carry):
-        first(order_of(k, place, long))
+    def step(k, carry):
+        @pl.when(k < long)
+        def _():
+            expert(k)
+
+        @pl.when(k == 1)
+        def _():
+            load_all.wait()
+            load_sg.wait()
+            load_sd.wait()
 
         @pl.when(k > 0)
         def _():
-            second(order_of(k - 1, place, long), False)
+            first(order_of(k - 1, place, long))
+
+        @pl.when(k > 1)
+        def _():
+            second(order_of(k - 2, place, long), False)
 
         return carry
 
-    lax.fori_loop(0, long, combine, 0)
+    lax.fori_loop(0, long + 1, step, 0)
     second(outer, True)
+    if direct:
+        last_copy().wait_recv()
+        total[:, far_lanes] += sidein[...].astype(f32)
+        last_copy().wait_send()
     out_ref[...] = (stream_ref[...].astype(f32) + total[...]).astype(bf16)
 
     for o in range(long):
@@ -744,10 +778,14 @@
         @pl.when(outer < o)
         def _():
             outer_copy(0, o).wait_send()
+            if direct:
+                side_copy(0, o).wait_send()
 
         @pl.when(outer > o)
         def _():
             outer_copy(1, o).wait_send()
+            if direct:
+                side_copy(1, o).wait_send()
 
         for j in range(1, columns):
             answer_copy(j, o).wait_send()
@@ -760,6 +798,7 @@
     long, short = line
     tokens, width = stream.shape
     count = arrived.shape[3]
+    direct = max(128, width // 8 // 128 * 128)
     hid, shid = (expert_down.shape[1], shared_down.shape[0])
     dma = pltpu.SemaphoreType.DMA
     block = (long, short, tokens, width)
@@ -785,6 +824,9 @@
             pltpu.VMEM((tokens, width), jnp.float32),
             pltpu.VMEM((columns * short * count, hid), bf16),
             pltpu.VMEM((tokens, shid), bf16),
+            pltpu.VMEM((long + 1, tokens, direct), bf16),
+            pltpu.VMEM((long, tokens, direct), bf16),
+            pltpu.VMEM((tokens, direct), bf16),
             dma((6,)),
             dma((2, long, short)),
             dma((2, long, short)),
@@ -792,6 +834,10 @@
             dma((2, long)),
             dma((columns, long)),
             dma((columns, long)),
+            dma((2, long)),
+            dma((2, long)),
+            dma,
+            dma,
         ],
         compiler_params=pltpu.CompilerParams(
             collective_id=1, has_side_effects=True, vmem_limit_bytes=60 * 2**20
@@ -822,14 +868,22 @@
     expert_gate_up,
     expert_down,
 ):
-    attended = attend(prefill_qkv, decode_qkv, cache_pool, page_table, cache_len)
     groups = lax.axis_size("exp")
     columns = lax.axis_size("req")
     line = (LINE, groups // LINE)
+    out_weights = [out_weight]
+    for k in range(1, line[1]):
+        turn = [
+            (o * line[1] + i, o * line[1] + (i + k) % line[1])
+            for o in range(line[0])
+            for i in range(line[1])
+        ]
+        out_weights.append(lax.ppermute(out_weight, "exp", turn))
+    attended = attend(prefill_qkv, decode_qkv, cache_pool, page_table, cache_len)
     plan = jnp.concatenate([routes.T.astype(jnp.float32), route_weight.T], axis=0)
     rows = row_limit(routes.shape, groups)
     stream, gathered, arrived, plan = front(
-        attended, out_weight, residual, norm_gain, plan, rows, line, columns
+        attended, out_weights, residual, norm_gain, plan, rows, line, columns
     )
     return back(
         arrived, gathered, expert_gate_up, expert_down, jnp.swapaxes(shared_gate_up, 1, 2),

time: 237 us -> 221 us (0.932); the launches traced: 233 us -> 220 us
  Pallas kernels: 224 us -> 205 us
  waiting for transfers between devices: 0 us -> 4.8 us
    pallas_call x1, Pallas kernels: 95.3 us -> 84.4 us  [back(): pl.pallas_call(functools.partial(back_kernel, line, columns), out_shape=j...]
    pallas_call x1, Pallas kernels: 116 us -> 108 us  [front(): pl.pallas_call(kernel, out_shape=(jax.ShapeDtypeStruct((tokens, width), b...]
    ppermute x0 -> x1, waiting for transfers between devices: none -> 4.8 us  [on_device(): out_weights.append(lax.ppermute(out_weight, 'exp', turn))]
  transfers between devices with their start and end apart: 0 -> 1, of which waited for: 0 -> 1; matrix products, arithmetic and copies ran while one was open for 0% -> 3% of each run, Pallas kernels for 0% -> 6%
where the time goes in v3:
time: 221 us; the launch traced here: 220 us
  Pallas kernels  205 us (93%)
  local copies, waits for them, and re-layouts  6.73 us (3%)
  waiting for transfers between devices  4.8 us (2%)
  other arithmetic  3.43 us (2%)
    pallas_call x1, Pallas kernels, front(): pl.pallas_call(kernel, out_shape=(jax.ShapeDtypeStruct((tokens, width), b...  108 us
    pallas_call x1, Pallas kernels, back(): pl.pallas_call(functools.partial(back_kernel, line, columns), out_shape=j...  84.4 us
    pallas_call x1, Pallas kernels, attend(): pl.pallas_call(functools.partial(attention_kernel, heads), grid=(steps,),...  12.2 us
    ppermute x1, waiting for transfers between devices, on_device(): out_weights.append(lax.ppermute(out_weight, 'exp', turn))  4.8 us
    unnamed x12, local copies, waits for them, and re-layouts  4.45 us
  transfers between devices with their start and end apart: 1, of which 1 were waited for; matrix products, arithmetic and copies ran while one was open for 3% of the time, Pallas kernels for 6%

profile of v3, /device:TPU:3, one launch (start us, length us, event | category | flops | bytes accessed | tf_op | source)
XLA Modules:
  0.0 219.8 jit_solution(3364740583098052577)
XLA Ops:
  0.0 0.0 collective-permute-start
  0.0 0.7 broadcast_subtract_fusion
  0.7 0.7 broadcast_compare_fusion
  1.5 1.3 select_reduce_fusion.1
  2.7 0.1 select_bitcast_fusion
  2.8 0.1 copy.18
  2.9 0.7 slice_bitcast_fusion
  3.7 0.0 copy-start
  3.7 1.4 copy-done
  5.1 0.0 copy-start.1
  5.1 0.0 copy-start.2
  5.1 0.0 copy-start.3
  5.1 12.2 %shard_map.145 = bf16[1040,256]{1,0:T(8,128)(2,1)S(1)} custom-call(bf16[2,3,512,256]{3,2,1,0:T(8,128)(2,1)S(1)} %copy-done, bf16[2,3,512,256]{3,2,1,0:T(8,128)(2,1)S(1)} %copy-done, bf16[2,3,512,256]{3,2,1,0:T(8,128)(2,1)S(1)} %copy-done, bf16[16,256]{1,0:T(8,128)(2,1)S(1)} %get-tuple-element.16.dq_ref, bf16[16,256]{1,0:T(8,128)(2,1)S(1)} %get-tuple-element.17.dk_ref, ...), custom_call_target="tpu_custom_call" | custom-call | flops 2000000000 | bytes 17825792 | tf_op jit(solution)/shard_map/pallas_call | solution.py:118
  17.3 0.9 reshape.108.att_ref
  18.2 0.0 copy-done.1
  18.2 0.6 reshape.110.gate_ref
  18.8 0.0 copy-done.2
  18.8 0.0 copy-done.3
  18.8 0.6 pad_maximum_fusion.refs_4_
  19.4 4.8 %collective-permute-done.refs_1_ = bf16[256,2048]{1,0:T(8,128)(2,1)S(1)} collective-permute-done((bf16[256,2048]{1,0:T(8,128)(2,1)}, bf16[256,2048]{1,0:T(8,128)(2,1)S(1)}, u32[]{:S(2)}, u32[]{:S(2)}) %collective-permute-start) | collective-permute-done | bytes 1048608 | tf_op jit(solution)/shard_map/ppermute | solution.py:881
  24.2 0.0 copy-start.4
  24.2 1.1 copy-done.4
  25.3 108.2 %shard_map.146 = (bf16[130,2048]{1,0:T(8,128)(2,1)}, bf16[4,2,130,2048]{3,2,1,0:T(8,128)(2,1)}, bf16[4,4,2,32,2048]{4,3,2,1,0:T(8,128)(2,1)}, f32[4,2,8,130]{3,2,1,0:T(8,128)}) custom-call(bf16[4,2,130,256]{3,2,1,0:T(8,128)(2,1)} %reshape.108.att_ref, bf16[256,2048]{1,0:T(8,128)(2,1)} %refs_0_.1, bf16[256,2048]{1,0:T(8,128)(2,1)} %copy-done.4, ...), custom_call_target="tpu_custom_call" | custom-call | flops 4000000000 | bytes 20000000 | tf_op jit(solution)/shard_map/pallas_call | solution.py:451
  133.5 84.4 %shard_map.147 = bf16[130,2048]{1,0:T(8,128)(2,1)} custom-call(bf16[4,4,2,32,2048]{4,3,2,1,0:T(8,128)(2,1)} %get-tuple-element.9.arr_ref, bf16[4,2,130,2048]{3,2,1,0:T(8,128)(2,1)} %get-tuple-element.10.all_ref, bf16[1,2,2048,1408]{3,2,1,0:T(8,128)(2,1)} %eg_ref.1, bf16[1,1408,2048]{2,1,0:T(8,128)(2,1)} %ed_ref.1, bf16[2,704,2048]{2,1,0:T(8,128)(2,1)} %bitcast.22, ...), custom_call_target="tpu_custom_call" | custom-call | flops 30000001024 | bytes 50000000 | tf_op jit(solution)/shard_map/pallas_call | solution.py:808
  217.9 1.9 copy.20
  (2 shorter events, 0.0 us)
Async XLA Ops:
  0.0 24.2 %collective-permute-start = (bf16[256,2048]{1,0:T(8,128)(2,1)}, bf16[256,2048]{1,0:T(8,128)(2,1)S(1)}, u32[]{:S(2)}, u32[]{:S(2)}) collective-permute-start(bf16[256,2048]{1,0:T(8,128)(2,1)} %refs_0_.1), channel_id=1, source_target_pairs={{0,1},{1,0},{2,3},{3,2},{4,5},{5,4},{6,7},{7,6},{8,9},{9,8},{10,11... | collective-permute-start | bytes 3145736 | tf_op jit(solution)/shard_map/ppermute | solution.py:881
  3.7 1.4 copy-start
  5.1 13.2 %copy-start.1 = (bf16[2048]{0:T(1024)(128)(2,1)S(1)}, bf16[2048]{0:T(1024)(128)(2,1)}, u32[]{:S(2)}) copy-start(bf16[2048]{0:T(1024)(128)(2,1)} %param.25) | copy-start | bytes 12292
  5.1 13.8 %copy-start.2 = (s32[130,4]{0,1:T(4,128)S(1)}, s32[130,4]{0,1:T(4,128)}, u32[]{:S(2)}) copy-start(s32[130,4]{0,1:T(4,128)} %param.26) | copy-start | bytes 6244
  5.1 13.8 %copy-start.3 = (f32[130,4]{0,1:T(4,128)S(1)}, f32[130,4]{0,1:T(4,128)}, u32[]{:S(2)}) copy-start(f32[130,4]{0,1:T(4,128)} %param.27) | copy-start | bytes 6244
  24.2 1.1 copy-start.4

commit v4 on v3

--- a/solution.py
+++ b/solution.py
@@ -202,8 +202,8 @@
 
 
 def front_kernel(
-    line, columns, att_ref, w_refs, res_ref, gain_ref, mine_ref, stream_ref, all_ref, arr_ref,
-    plan_ref, attin, column, rout, total, pack, isend, irecv, osend, orecv, asend, arecv, bsend,
+    line, columns, att_ref, w_refs, res_ref, gain_ref, mine_ref, gate_ref, sg_ref, sd_ref,
+    stream_ref, shared_ref, arr_ref, plan_ref, all_ref, sg, sd, shidden, load, attin, column, rout, total, pack, isend, irecv, osend, orecv, asend, arecv, bsend,
     brecv, ysend, yrecv, psend, precv,
 ):
     long, short = line
@@ -214,6 +214,10 @@
     outer, inner = place
     f32, bf16 = (jnp.float32, jnp.bfloat16)
     direct = all_ref.shape[3] // 8 // 128 * 128 if short == 2 else 0
+    load_sg = pltpu.make_async_copy(sg_ref, sg, load.at[0])
+    load_sd = pltpu.make_async_copy(sd_ref, sd, load.at[1])
+    load_sg.start()
+    load_sd.start()
     greet(place, line, groups, columns, True)
 
     def rows_copy(k, o):
@@ -331,6 +335,30 @@
         for k in range(1, columns):
             to_column(k, o, i).start()
         arr_ref[o, me, i] = pack[o, i, me]
+
+    def shared(i, o):
+        x = all_ref[o, i]
+        scale = jax.nn.sigmoid(
+            jnp.sum(x.astype(f32) * gate_ref[...].astype(f32), axis=-1, keepdims=True)
+        )
+        for lower, upper in tiles(sg.shape[1], 256):
+            gate = lax.dot_general(
+                x, sg[0, lower:upper], ROWS_BY_ROWS, preferred_element_type=f32
+            )
+            up = lax.dot_general(
+                x, sg[1, lower:upper], ROWS_BY_ROWS, preferred_element_type=f32
+            )
+            shidden[:, lower:upper] = (jax.nn.silu(gate) * up).astype(bf16)
+        for lower, upper in tiles(all_ref.shape[3], 512):
+            down = jnp.dot(shidden[...], sd[:, lower:upper], preferred_element_type=f32)
+            shared_ref[o, i, :, lower:upper] = (scale * down).astype(bf16)
+
+    def share(o, distance, side):
+        def one(i, carry):
+            shared(i, o)
+            return carry
+
+        lax.fori_loop(0, short, one, 0)
 
     def onward(o, i, distance, side, lanes):
         for way, ahead in ((0, outer < long - 1), (1, outer > 0)):
@@ -376,6 +404,12 @@
             near(place, long, step, spread)
         if step > 0:
             near(place, long, step - 1, across)
+        if step == 1:
+            load_sg.wait()
+            load_sd.wait()
+        if step > 1:
+            near(place, long, step - 2, share)
+    near(place, long, long - 1, share)
 
     for k in range(1, groups):
         plan_copy(k).wait_send()
@@ -436,7 +470,10 @@
             body(outer - distance, distance, 1)
 
 
-def front(attended, out_weights, residual, norm_gain, plan, rows, line, columns):
+def front(
+    attended, out_weights, residual, norm_gain, plan, shared_gate_up, shared_down, shared_gate,
+    rows, line, columns,
+):
     long, short = line
     tokens, width = residual.shape
     depth = out_weights[0].shape[0]
@@ -456,9 +493,14 @@
             jax.ShapeDtypeStruct((long, columns, short, rows, width), bf16),
             jax.ShapeDtypeStruct((long, short) + plan.shape, jnp.float32),
         ),
-        in_specs=[vmem] * (4 + short),
+        in_specs=[vmem] * (5 + short) + [pl.BlockSpec(memory_space=pl.ANY)] * 2,
         out_specs=(vmem, vmem, vmem, vmem),
         scratch_shapes=[
+            pltpu.VMEM(block, bf16),
+            pltpu.VMEM(shared_gate_up.shape, bf16),
+            pltpu.VMEM(shared_down.shape, bf16),
+            pltpu.VMEM((tokens, shared_down.shape[0]), bf16),
+            dma((2,)),
             pltpu.VMEM((short, long, tokens, depth), bf16),
             pltpu.VMEM((long, tokens, width), bf16),
             pltpu.VMEM((long + 1, tokens, width), bf16),
@@ -485,7 +527,8 @@
         ),
     )(
         attended.reshape(long, short, tokens, depth), *out_weights, residual,
-        norm_gain.reshape(1, width), plan,
+        norm_gain.reshape(1, width), plan, shared_gate.reshape(1, width), shared_gate_up,
+        shared_down,
     )
 
 
@@ -504,9 +547,8 @@
 
 
 def back_kernel(
-    line, columns, arr_ref, all_ref, eg_ref, ed_ref, sg_ref, sd_ref, gate_ref, plan_ref,
-    stream_ref, out_ref, rows, part, eg, ed, sg, sd, ret, rin, rout, column, total, hidden,
-    shidden, sideout, sidecol, sidein, load, isend, irecv, osend, orecv, ysend, yrecv, ssend,
+    line, columns, arr_ref, shared_ref, eg_ref, ed_ref, plan_ref, stream_ref, out_ref, rows, part,
+    eg, ed, ret, rin, rout, column, total, hidden, sideout, sidecol, sidein, load, isend, irecv, osend, orecv, ysend, yrecv, ssend,
     srecv, tsend, trecv,
 ):
     long, short = line
@@ -520,14 +562,27 @@
     far_lanes = slice(width - direct, width)
     bf16, f32 = (jnp.bfloat16, jnp.float32)
 
-    load_rows = pltpu.make_async_copy(arr_ref, rows, load.at[0])
-    load_eg = pltpu.make_async_copy(eg_ref.at[0], eg, load.at[1])
-    load_ed = pltpu.make_async_copy(ed_ref.at[0], ed, load.at[2])
-    load_sg = pltpu.make_async_copy(sg_ref, sg, load.at[3])
-    load_sd = pltpu.make_async_copy(sd_ref, sd, load.at[4])
-    load_all = pltpu.make_async_copy(all_ref, part, load.at[5])
-    for copy in (load_rows, load_eg, load_ed):
-        copy.start()
+    cuts = tiles(eg.shape[2], 256)
+
+    def load_rows(k):
+        o = order_of(k, place, long)
+        return pltpu.make_async_copy(arr_ref.at[o], rows.at[o], load.at[2 + k])
+
+    def load_eg(t):
+        lanes = slice(*cuts[t])
+        return pltpu.make_async_copy(
+            eg_ref.at[0, :, :, lanes], eg.at[:, :, lanes], load.at[2 + long + t]
+        )
+
+    load_ed = pltpu.make_async_copy(ed_ref.at[0], ed, load.at[0])
+    load_shared = pltpu.make_async_copy(shared_ref, part, load.at[1])
+    load_rows(0).start()
+    for t in range(len(cuts)):
+        load_eg(t).start()
+    load_ed.start()
+    for k in range(1, long):
+        load_rows(k).start()
+    load_shared.start()
     greet(place, line, long * short, columns, False)
 
     def answer_copy(k, o):
@@ -541,15 +596,15 @@
             device_id_type=MESH,
         )
 
-    load_rows.wait()
-    load_eg.wait()
-    for copy in (load_all, load_sg, load_sd):
-        copy.start()
-
     def expert(k):
         o = order_of(k, place, long)
+        load_rows(k).wait()
         x = rows[o].reshape(hidden.shape[0], width)
-        for lower, upper in tiles(eg.shape[2], 256):
+        for t, (lower, upper) in enumerate(cuts):
+            @pl.when(k == 0)
+            def _():
+                load_eg(t).wait()
+
             gate = jnp.dot(x, eg[0, :, lower:upper], preferred_element_type=f32)
             up = jnp.dot(x, eg[1, :, lower:upper], preferred_element_type=f32)
             hidden[:, lower:upper] = (jax.nn.silu(gate) * up).astype(bf16)
@@ -639,22 +694,6 @@
         return i, ok, behind
 
     def fill(o):
-        for i in range(short):
-            x = part[o, i]
-            scale = jax.nn.sigmoid(
-                jnp.sum(x.astype(f32) * gate_ref[...].astype(f32), axis=-1, keepdims=True)
-            )
-            for lower, upper in tiles(sg.shape[1], 256):
-                gate = lax.dot_general(
-                    x, sg[0, lower:upper], ROWS_BY_ROWS, preferred_element_type=f32
-                )
-                up = lax.dot_general(
-                    x, sg[1, lower:upper], ROWS_BY_ROWS, preferred_element_type=f32
-                )
-                shidden[:, lower:upper] = (jax.nn.silu(gate) * up).astype(bf16)
-            for lower, upper in tiles(width, 512):
-                down = jnp.dot(shidden[...], sd[:, lower:upper], preferred_element_type=f32)
-                part[o, i, :, lower:upper] = (scale * down).astype(bf16)
         for j in range(1, columns):
             answer_copy(j, o).wait_recv()
         for i in range(short):
@@ -743,9 +782,7 @@
 
         @pl.when(k == 1)
         def _():
-            load_all.wait()
-            load_sg.wait()
-            load_sd.wait()
+            load_shared.wait()
 
         @pl.when(k > 0)
         def _():
@@ -792,14 +829,13 @@
 
 
 def back(
-    arrived, gathered, expert_gate_up, expert_down, shared_gate_up, shared_down, shared_gate,
-    plan, stream, line, columns,
+    arrived, shared, expert_gate_up, expert_down, plan, stream, line, columns,
 ):
     long, short = line
     tokens, width = stream.shape
     count = arrived.shape[3]
     direct = max(128, width // 8 // 128 * 128)
-    hid, shid = (expert_down.shape[1], shared_down.shape[0])
+    hid = expert_down.shape[1]
     dma = pltpu.SemaphoreType.DMA
     block = (long, short, tokens, width)
     vmem = pl.BlockSpec(memory_space=pltpu.VMEM)
@@ -808,26 +844,23 @@
     return pl.pallas_call(
         functools.partial(back_kernel, line, columns),
         out_shape=jax.ShapeDtypeStruct((tokens, width), bf16),
-        in_specs=[hbm] * 6 + [vmem] * 3,
+        in_specs=[hbm] * 4 + [vmem] * 2,
         out_specs=vmem,
         scratch_shapes=[
             pltpu.VMEM(arrived.shape, bf16),
             pltpu.VMEM(block, bf16),
             pltpu.VMEM(expert_gate_up.shape[1:], bf16),
             pltpu.VMEM(expert_down.shape[1:], bf16),
-            pltpu.VMEM(shared_gate_up.shape, bf16),
-            pltpu.VMEM(shared_down.shape, bf16),
             pltpu.VMEM(arrived.shape, bf16),
             pltpu.VMEM((long, short + 1, tokens, width), bf16),
             pltpu.VMEM((long + 1, tokens, width), bf16),
             pltpu.VMEM((long, tokens, width), bf16),
             pltpu.VMEM((tokens, width), jnp.float32),
             pltpu.VMEM((columns * short * count, hid), bf16),
-            pltpu.VMEM((tokens, shid), bf16),
             pltpu.VMEM((long + 1, tokens, direct), bf16),
             pltpu.VMEM((long, tokens, direct), bf16),
             pltpu.VMEM((tokens, direct), bf16),
-            dma((6,)),
+            dma((2 + long + len(tiles(hid, 256)),)),
             dma((2, long, short)),
             dma((2, long, short)),
             dma((2, long)),
@@ -846,8 +879,7 @@
             flops=3 * 10**10, bytes_accessed=5 * 10**7, transcendentals=0
         ),
     )(
-        arrived, gathered, expert_gate_up, expert_down, shared_gate_up, shared_down,
-        shared_gate.reshape(1, width), plan, stream,
+        arrived, shared, expert_gate_up, expert_down, plan, stream,
     )
 
 
@@ -882,12 +914,12 @@
     attended = attend(prefill_qkv, decode_qkv, cache_pool, page_table, cache_len)
     plan = jnp.concatenate([routes.T.astype(jnp.float32), route_weight.T], axis=0)
     rows = row_limit(routes.shape, groups)
-    stream, gathered, arrived, plan = front(
-        attended, out_weights, residual, norm_gain, plan, rows, line, columns
+    stream, shared, arrived, plan = front(
+        attended, out_weights, residual, norm_gain, plan, jnp.swapaxes(shared_gate_up, 1, 2),
+        shared_down, shared_gate, rows, line, columns,
     )
     return back(
-        arrived, gathered, expert_gate_up, expert_down, jnp.swapaxes(shared_gate_up, 1, 2),
-        shared_down, shared_gate, plan, stream, line, columns,
+        arrived, shared, expert_gate_up, expert_down, plan, stream, line, columns
     )
 
 

time: 221 us -> 219 us (level)
    unnamed x12 -> x10, local copies, waits for them, and re-layouts: 4.45 us -> 4.43 us
where the time goes in v4:
time: 219 us
  Pallas kernels  204 us (93%)
  local copies, waits for them, and re-layouts  7.4 us (3%)
  waiting for transfers between devices  4.15 us (2%)
  other arithmetic  3.42 us (2%)
    pallas_call x1, Pallas kernels, front(): pl.pallas_call(kernel, out_shape=(jax.ShapeDtypeStruct((tokens, width), b...  108 us
    pallas_call x1, Pallas kernels, back(): pl.pallas_call(functools.partial(back_kernel, line, columns), out_shape=j...  83.4 us
    pallas_call x1, Pallas kernels, attend(): pl.pallas_call(functools.partial(attention_kernel, heads), grid=(steps,),...  12.2 us
    unnamed x10, local copies, waits for them, and re-layouts  4.43 us
  transfers between devices with their start and end apart: 1, of which 1 were waited for; matrix products, arithmetic and copies ran while one was open for 3% of the time, Pallas kernels for 6%

profile of v4, /device:TPU:3, one launch (start us, length us, event | category | flops | bytes accessed | tf_op | source)
XLA Modules:
  0.0 218.9 jit_solution(4877763751325501478)
XLA Ops:
  0.0 0.0 collective-permute-start
  0.0 0.7 broadcast_compare_fusion
  0.7 0.7 broadcast_subtract_fusion
  1.5 1.3 reshape.110.refs_5_
  2.8 1.3 select_reduce_fusion.1
  4.0 0.1 select_bitcast_fusion
  4.1 0.1 copy.18
  4.2 0.7 slice_bitcast_fusion
  4.9 0.0 copy-start
  4.9 1.4 copy-done
  6.4 0.0 copy-start.1
  6.4 0.0 copy-start.2
  6.4 12.2 %shard_map.145 = bf16[1040,256]{1,0:T(8,128)(2,1)S(1)} custom-call(bf16[2,3,512,256]{3,2,1,0:T(8,128)(2,1)S(1)} %copy-done, bf16[2,3,512,256]{3,2,1,0:T(8,128)(2,1)S(1)} %copy-done, bf16[2,3,512,256]{3,2,1,0:T(8,128)(2,1)S(1)} %copy-done, bf16[16,256]{1,0:T(8,128)(2,1)S(1)} %get-tuple-element.16.dq_ref, bf16[16,256]{1,0:T(8,128)(2,1)S(1)} %get-tuple-element.17.dk_ref, ...), custom_call_target="tpu_custom_call" | custom-call | flops 2000000000 | bytes 17825792 | tf_op jit(solution)/shard_map/pallas_call | solution.py:118
  18.5 0.9 reshape.108.att_ref
  19.5 0.0 copy-done.1
  19.5 0.0 copy-done.2
  19.5 0.6 pad_maximum_fusion.refs_4_
  20.1 4.1 %collective-permute-done.refs_1_ = bf16[256,2048]{1,0:T(8,128)(2,1)S(1)} collective-permute-done((bf16[256,2048]{1,0:T(8,128)(2,1)}, bf16[256,2048]{1,0:T(8,128)(2,1)S(1)}, u32[]{:S(2)}, u32[]{:S(2)}) %collective-permute-start) | collective-permute-done | bytes 1048608 | tf_op jit(solution)/shard_map/ppermute | solution.py:913
  24.2 0.0 copy-start.3
  24.2 1.0 copy-done.3
  25.3 108.3 %shard_map.146 = (bf16[130,2048]{1,0:T(8,128)(2,1)}, bf16[4,2,130,2048]{3,2,1,0:T(8,128)(2,1)}, bf16[4,4,2,32,2048]{4,3,2,1,0:T(8,128)(2,1)}, f32[4,2,8,130]{3,2,1,0:T(8,128)}) custom-call(bf16[4,2,130,256]{3,2,1,0:T(8,128)(2,1)} %reshape.108.att_ref, bf16[256,2048]{1,0:T(8,128)(2,1)} %refs_0_.1, bf16[256,2048]{1,0:T(8,128)(2,1)} %copy-done.3, ...), custom_call_target="tpu_custom_call" | custom-call | flops 4000000000 | bytes 20000000 | tf_op jit(solution)/shard_map/pallas_call | solution.py:488
  133.6 83.4 %shard_map.147 = bf16[130,2048]{1,0:T(8,128)(2,1)} custom-call(bf16[4,4,2,32,2048]{4,3,2,1,0:T(8,128)(2,1)} %get-tuple-element.9.arr_ref, bf16[4,2,130,2048]{3,2,1,0:T(8,128)(2,1)} %get-tuple-element.10.shared_ref, bf16[1,2,2048,1408]{3,2,1,0:T(8,128)(2,1)} %eg_ref.1, bf16[1,1408,2048]{2,1,0:T(8,128)(2,1)} %ed_ref.1, ...), custom_call_target="tpu_custom_call" | custom-call | flops 30000001024 | bytes 50000000 | tf_op jit(solution)/shard_map/pallas_call | solution.py:844
  217.0 1.9 copy.20
  (2 shorter events, 0.0 us)
Async XLA Ops:
  0.0 24.2 %collective-permute-start = (bf16[256,2048]{1,0:T(8,128)(2,1)}, bf16[256,2048]{1,0:T(8,128)(2,1)S(1)}, u32[]{:S(2)}, u32[]{:S(2)}) collective-permute-start(bf16[256,2048]{1,0:T(8,128)(2,1)} %refs_0_.1), channel_id=1, source_target_pairs={{0,1},{1,0},{2,3},{3,2},{4,5},{5,4},{6,7},{7,6},{8,9},{9,8},{10,11... | collective-permute-start | bytes 3145736 | tf_op jit(solution)/shard_map/ppermute | solution.py:913
  4.9 1.4 copy-start
  6.4 13.1 %copy-start.1 = (s32[130,4]{0,1:T(4,128)S(1)}, s32[130,4]{0,1:T(4,128)}, u32[]{:S(2)}) copy-start(s32[130,4]{0,1:T(4,128)} %param.26) | copy-start | bytes 6244
  6.4 13.1 %copy-start.2 = (f32[130,4]{0,1:T(4,128)S(1)}, f32[130,4]{0,1:T(4,128)}, u32[]{:S(2)}) copy-start(f32[130,4]{0,1:T(4,128)} %param.27) | copy-start | bytes 6244
  24.2 1.0 copy-start.3
